TPU v7x, 256 devices: a whole 4x4x8 slice. The times are simulated.
256 devices in a mesh: pop: 8 (over z), seq: 32 (over y, x, core).
Axes of the slice: x: 4, y: 4, z: 8, core: 2. Of those that a mesh axis runs over, the one named last changes fastest.
Arguments:
- queries: bfloat16 [16384, 2048], P(('pop', 'seq')), parts along dimension 0, may hold values from -12 to 12
- keys: bfloat16 [131072, 2048], P(('pop', 'seq')), parts along dimension 0, may hold values from -4 to 4
- values: bfloat16 [131072, 2048], P(('pop', 'seq')), parts along dimension 0, may hold values from -6 to 6
- cotangent: bfloat16 [16384, 2048], P(('pop', 'seq')), parts along dimension 0, may hold values from -6 to 6
- neighbour_ids: int32 [256, 8], P('pop'), parts along dimension 0, may hold values from 0 to 127, as said below
- neighbour_counts: int32 [256], P('pop'), parts along dimension 0, may hold values from 2 to 8
Outputs:
- attended: bfloat16 [16384, 2048], P(('pop', 'seq')), parts along dimension 0
- query_grad: bfloat16 [16384, 2048], P(('pop', 'seq')), parts along dimension 0
- key_grad: bfloat16 [131072, 2048], P(('pop', 'seq')), parts along dimension 0
- value_grad: bfloat16 [131072, 2048], P(('pop', 'seq')), parts along dimension 0
There are 8 independent parts, one for each index of `pop`. A program takes and returns all parts, laid end to end along the dimension named above; each array names one. Nothing has to cross between parts.
Inputs may be any that keep to these rules, and one draw needn't show every extreme that they name: `neighbour_ids`: the entries of one group's list are distinct; each names a neighbour held by the index of seq that holds the group or by the next index, the last index's next being index 0 (neighbour n is held by index n // 4, group c by index c); entries at or past the group's count are ignored.
All inputs are finite; a program needn't handle non-finite values.
Results may differ from a plain program's by a relative error of at most 0.04.
Values may be sent and summed in bfloat16 or wider, within the bound.
No kernel may reach another device: no remote copies, remote signals or barrier semaphores. Data moves between devices by JAX's collectives and lax.ppermute only.
A program may use at most 128 MiB of HBM per device.

v0:
```python
import math

import jax
import jax.numpy as jnp
from jax import lax
from jax.sharding import PartitionSpec as P

HEADS = 16
HD = 128
GROUP = 64
NLEN = 128
SLOTS = 8


masked_low = -1e30


def passed_along(block, axis, distance):
    devices = range(lax.axis_size(axis))
    route = [((i - distance) % len(devices), i) for i in devices]
    return lax.ppermute(block, axis, route)


def block_partial(scores, keymask, vals):
    wide = keymask[:, None, None, :]
    peaks = jnp.max(jnp.where(wide, scores, masked_low), axis=-1)
    weights = jnp.where(wide, jnp.exp(scores - peaks[..., None]), 0.0)
    numer = jnp.einsum(
        "chik,khd->chid", weights.astype(jnp.bfloat16), vals, preferred_element_type=jnp.float32
    )
    return (numer, peaks, jnp.sum(weights, axis=-1))


def merge_blocks(numer, peaks, totals):
    alive = totals > 0.0
    top = jnp.max(jnp.where(alive, peaks, masked_low), axis=0)
    factor = jnp.where(alive, jnp.exp(jnp.where(alive, peaks - top, masked_low)), 0.0)
    denom = jnp.sum(factor * totals, axis=0)
    attended = jnp.sum(factor[..., None] * numer, axis=0) / denom[..., None]
    return (attended, top + jnp.log(denom))


def live_keys(group_ids, group_counts, named):
    slot = jnp.arange(SLOTS, dtype=jnp.int32)
    used = slot[None, :] < group_counts[:, None]
    hit = jnp.any((group_ids[:, :, None] == named[None, None, :]) & used[:, :, None], axis=1)
    return jnp.repeat(hit, NLEN, axis=1)


def per_device(queries, keys, values, cotangent, neighbour_ids, neighbour_counts):
    scale = 1.0 / math.sqrt(HD)
    index = lax.axis_index("seq")
    holders = lax.axis_size("seq")
    following = (index + 1) % holders
    tok_rows, width = queries.shape
    group_count = tok_rows // GROUP
    pool_rows = keys.shape[0]
    pool_count = pool_rows // NLEN
    counter = jnp.arange(pool_count, dtype=jnp.int32)
    q_heads = queries.reshape(group_count, GROUP, HEADS, HD)
    g_heads = cotangent.reshape(group_count, GROUP, HEADS, HD)
    start = index * group_count
    own_ids = lax.dynamic_slice_in_dim(neighbour_ids, start, group_count, 0)
    own_counts = lax.dynamic_slice_in_dim(neighbour_counts, start, group_count, 0)
    named = jnp.concatenate([index * pool_count + counter, following * pool_count + counter])
    keymask = live_keys(own_ids, own_counts, named)
    keymask = jnp.transpose(keymask.reshape(group_count, 2, pool_rows), (1, 0, 2))
    stacked = jnp.stack([keys, values])
    arrived = passed_along(stacked, "seq", -1)
    k_win = jnp.stack([keys, arrived[0]]).reshape(2, pool_rows, HEADS, HD)
    v_win = jnp.stack([values, arrived[1]]).reshape(2, pool_rows, HEADS, HD)
    scores = (
        jnp.einsum("cihd,bkhd->bchik", q_heads, k_win, preferred_element_type=jnp.float32) * scale
    )
    numer, peaks, totals = jax.vmap(block_partial)(scores, keymask, v_win)
    attended, lse = merge_blocks(numer, peaks, totals)
    out = jnp.transpose(attended, (0, 2, 1, 3)).reshape(tok_rows, width).astype(jnp.bfloat16)
    delta = jnp.einsum(
        "cihd,cihd->chi",
        g_heads,
        out.reshape(group_count, GROUP, HEADS, HD),
        preferred_element_type=jnp.float32,
    )
    wide = keymask[:, :, None, None, :]
    prob = jnp.where(wide, jnp.exp(scores - lse[None, ..., None]), 0.0)
    dv_win = jnp.einsum(
        "bchik,cihd->bkhd", prob.astype(jnp.bfloat16), g_heads, preferred_element_type=jnp.float32
    )
    dprob = jnp.einsum("cihd,bkhd->bchik", g_heads, v_win, preferred_element_type=jnp.float32)
    dscore = (prob * (dprob - delta[None, ..., None])).astype(jnp.bfloat16)
    query_sum = (
        jnp.einsum("bchik,bkhd->cihd", dscore, k_win, preferred_element_type=jnp.float32) * scale
    )
    query_grad = query_sum.reshape(tok_rows, width).astype(jnp.bfloat16)
    dk_win = (
        jnp.einsum("bchik,cihd->bkhd", dscore, q_heads, preferred_element_type=jnp.float32) * scale
    )
    blocks = jnp.stack([dk_win, dv_win], axis=1).reshape(2, 2, pool_rows, width)
    total = blocks[0] + passed_along(blocks[1], "seq", 1)
    key_grad = total[0].astype(jnp.bfloat16)
    value_grad = total[1].astype(jnp.bfloat16)
    return (out, query_grad, key_grad, value_grad)


def solution(mesh):
    in_specs = (
        P(("pop", "seq"), None),
        P(("pop", "seq"), None),
        P(("pop", "seq"), None),
        P(("pop", "seq"), None),
        P("pop", None),
        P("pop"),
    )
    out_specs = (
        P(("pop", "seq"), None),
        P(("pop", "seq"), None),
        P(("pop", "seq"), None),
        P(("pop", "seq"), None),
    )
    return jax.shard_map(
        per_device, mesh=mesh, in_specs=in_specs, out_specs=out_specs, check_vma=False
    )
```

profile of v0, /device:TPU:160, one launch (start us, length us, event | category | flops | bytes accessed | tf_op | source)
XLA Modules:
  0.0 211.1 jit_solution(1492271197349297561)
XLA Ops:
  0.6 3.9 %copy.76 = bf16[512,2048]{0,1:T(8,128)(2,1)} copy(bf16[512,2048]{1,0:T(8,128)(2,1)} %param.7) | data formatting | bytes 4194304 | tf_op args[1]
  4.6 2.9 %copy.78 = bf16[512,2048]{0,1:T(8,128)(2,1)S(1)} copy(bf16[512,2048]{1,0:T(8,128)(2,1)} %param.8) | data formatting | bytes 4194304 | tf_op args[2]
  7.5 4.0 %pad_maximum_fusion.1 = bf16[2,512,2048]{1,2,0:T(8,128)(2,1)} fusion(bf16[1,512,2048]{1,2,0:T(8,128)(2,1)S(1)} %bitcast.138, bf16[1,512,2048]{1,2,0:T(8,128)(2,1)} %bitcast.140), kind=kLoop, calls=%fused_computation.6 | loop fusion | flops 2097152 | bytes 8388608 | tf_op jit(solution)/shard_map/stack | solution.py:68
  11.4 4.6 %collective-permute-start = (bf16[2,512,2048]{1,2,0:T(8,128)(2,1)}, bf16[2,512,2048]{1,2,0:T(8,128)(2,1)}, u32[]{:S(2)}, u32[]{:S(2)}) collective-permute-start(bf16[2,512,2048]{1,2,0:T(8,128)(2,1)} %pad_maximum_fusion.1), channel_id=1, source_target_pairs={{1,0},{2,1},{3,2},{4,3},{5,4},{6,5},{7,6},{8,7},{9,8},{10,9},{11,1... | collective-permute-start | bytes 12582920 | tf_op jit(solution)/shard_map/ppermute | solution.py:21
  16.1 0.6 dynamic_slice.10
  16.9 0.7 iota_compare_fusion
  18.0 3.9 %copy.79 = bf16[1,512,16,128]{3,1,0,2:T(8,128)(2,1)} copy(bf16[1,512,16,128]{1,3,2,0:T(8,128)(2,1)} %bitcast.141) | data formatting | bytes 4194304 | tf_op jit(solution)/shard_map/stack | solution.py:70
  21.9 2.4 %copy.84 = bf16[1,512,16,128]{3,1,2,0:T(8,128)(2,1)} copy(bf16[1,512,16,128]{1,3,2,0:T(8,128)(2,1)S(1)} %bitcast.139) | data formatting | bytes 4194304 | tf_op jit(solution)/shard_map/stack | solution.py:71
  24.3 38.1 %collective-permute-done = bf16[2,512,2048]{1,2,0:T(8,128)(2,1)} collective-permute-done((bf16[2,512,2048]{1,2,0:T(8,128)(2,1)}, bf16[2,512,2048]{1,2,0:T(8,128)(2,1)}, u32[]{:S(2)}, u32[]{:S(2)}) %collective-permute-start) | collective-permute-done | bytes 4194336 | tf_op jit(solution)/shard_map/ppermute | solution.py:21
  62.4 3.8 %fusion.49 = (bf16[1,512,2048]{1,2,0:T(8,128)(2,1)}, bf16[1,512,2048]{1,2,0:T(8,128)(2,1)S(1)}) fusion(bf16[2,512,2048]{1,2,0:T(8,128)(2,1)} %collective-permute-done), kind=kLoop, calls=%fused_computation.74 | loop fusion | bytes 8388608 | tf_op jit(solution)/shard_map/slice | solution.py:71
  66.2 3.9 %copy.85 = bf16[1,512,16,128]{3,1,2,0:T(8,128)(2,1)} copy(bf16[1,512,16,128]{1,3,2,0:T(8,128)(2,1)} %bitcast.143) | data formatting | bytes 4194304 | tf_op jit(solution)/shard_map/stack | solution.py:71
  70.2 2.4 %copy.80 = bf16[1,512,16,128]{3,1,0,2:T(8,128)(2,1)} copy(bf16[1,512,16,128]{1,3,2,0:T(8,128)(2,1)S(1)} %bitcast.142) | data formatting | bytes 4194304 | tf_op jit(solution)/shard_map/stack | solution.py:70
  72.5 3.9 %fusion.2 = (f32[2,16,64]{2,0,1:T(2,128)S(1)}, f32[16,2,512,64]{2,3,1,0:T(8,128)S(1)}) fusion(pred[2,512]{1,0:T(4,128)(4,1)S(1)} %bitcast.155, bf16[64,16,128,1]{2,1,0,3:T(8,128)(2,1)S(1)} %bitcast.149, bf16[1,512,16,128]{3,1,0,2:T(8,128)(2,1)} %copy.80, bf16[1,512,16,128]{3,1,0,2:T(8,128)(2,1)} %copy.79), kind=kOutput, calls=%fused_computation.15 | convolution fusion | flops 273676288 | bytes 8659968 | tf_op jit(solution)/shard_map/cihd,bkhd->bchik/dot_general | solution.py:73
  76.4 1.3 fusion.14
  77.9 1.6 copy-done.5
  79.5 0.6 copy-done.6
  80.2 1.1 fusion.32
  81.3 0.2 bitcast_convert_fusion
  81.5 0.4 multiply_reduce_fusion
  81.9 3.7 %convolution_bitcast_fusion = f32[2,1,512,16,128]{2,4,0,3,1:T(8,128)S(1)} fusion(f32[16,2,512,64]{2,3,1,0:T(8,128)} %copy-done.2, f32[16,64]{1,0:T(8,128)S(1)} %log_add_fusion, pred[2,512]{1,0:T(4,128)(4,1)S(1)} %bitcast.157, bf16[64,16,128,1]{2,1,0,3:T(8,128)(2,1)S(1)} %bitcast.145), kind=kOutput, calls=%fused_computation.22 | convolution fusion | flops 272629760 | bytes 12850176 | tf_op jit(solution)/shard_map/bchik,cihd->bkhd/dot_general | solution.py:86
  85.6 0.4 copy-done.7
  86.1 1.8 fusion.17
  87.9 1.3 multiply_bitcast_fusion
  89.3 6.7 %pad_maximum_fusion = (f32[1,2,512,16,128]{2,4,0,3,1:T(8,128)}, f32[1,2,512,16,128]{2,4,0,3,1:T(8,128)}) fusion(f32[2,1,512,16,128]{2,4,0,3,1:T(8,128)S(1)} %convolution_bitcast_fusion, f32[2,1,512,16,128]{2,4,0,3,1:T(8,128)S(1)} %multiply_bitcast_fusion), kind=kLoop, calls=%fused_computation.3 | loop fusion | flops 4194304 | bytes 33554432 | tf_op jit(solution)/shard_map/stack | solution.py:98
  96.0 8.8 %copy.93 = f32[2,512,2048]{2,1,0:T(8,128)} copy(f32[2,512,2048]{1,2,0:T(8,128)} %bitcast.137) | data formatting | bytes 16777216 | tf_op jit(solution)/shard_map/squeeze | solution.py:99
  104.9 3.2 %fusion.38 = bf16[1,64,16,128]{3,1,2,0:T(8,128)(2,1)S(1)} fusion(bf16[2,16,64,512]{3,2,0,1:T(8,128)(2,1)} %copy-done.8, bf16[1,512,16,128]{3,1,0,2:T(8,128)(2,1)} %copy.80, bf16[1,512,16,128]{3,1,0,2:T(8,128)(2,1)S(1)} %copy-done.4), kind=kOutput, calls=%fused_computation.45 | convolution fusion | flops 277086208 | bytes 6553600 | tf_op jit(solution)/shard_map/bchik,bkhd->cihd/dot_general | solution.py:92
  108.2 0.8 copy.146
  109.2 0.8 copy.147
  109.9 8.7 %copy.94 = f32[2,512,2048]{2,1,0:T(8,128)} copy(f32[2,512,2048]{1,2,0:T(8,128)} %bitcast.136) | data formatting | bytes 16777216 | tf_op jit(solution)/shard_map/squeeze | solution.py:99
  118.6 82.9 %collective-permute-done.1 = f32[2,512,2048]{2,1,0:T(8,128)} collective-permute-done((f32[2,512,2048]{2,1,0:T(8,128)}, f32[2,512,2048]{2,1,0:T(8,128)}, u32[]{:S(2)}, u32[]{:S(2)}) %collective-permute-start.1) | collective-permute-done | bytes 8388640 | tf_op jit(solution)/shard_map/ppermute | solution.py:21
  201.5 7.2 %add_convert_fusion = bf16[2,512,2048]{2,1,0:T(8,128)(2,1)S(1)} fusion(f32[2,512,2048]{2,1,0:T(8,128)} %copy.94, f32[2,512,2048]{2,1,0:T(8,128)} %collective-permute-done.1), kind=kLoop, calls=%fused_computation.4 | loop fusion | flops 4194304 | bytes 20971520 | tf_op jit(solution)/shard_map/convert.1
  208.8 2.3 %slice_bitcast_fusion = (bf16[512,2048]{1,0:T(8,128)(2,1)}, bf16[512,2048]{1,0:T(8,128)(2,1)}) fusion(bf16[2,512,2048]{2,1,0:T(8,128)(2,1)S(1)} %add_convert_fusion), kind=kLoop, calls=%fused_computation.31 | loop fusion | bytes 8388608 | tf_op jit(solution)/shard_map/convert_element_type | solution.py:101
  (38 shorter events, 1.3 us)
Async XLA Ops:
  0.6 16.0 %copy-start = (s32[32,8]{0,1:T(8,128)S(1)}, s32[32,8]{0,1:T(8,128)}, u32[]{:S(2)}) copy-start(s32[32,8]{0,1:T(8,128)} %param.10) | copy-start | bytes 3076
  7.4 8.6 %copy-start.11 = (s32[32]{0:T(128)S(1)}, s32[32]{0:T(128)}, u32[]{:S(2)}) copy-start(s32[32]{0:T(128)} %param.11) | copy-start | bytes 388
  7.5 10.4 %copy-start.9 = (bf16[64,2048]{1,0:T(8,128)(2,1)S(1)}, bf16[64,2048]{1,0:T(8,128)(2,1)}, u32[]{:S(2)}) copy-start(bf16[64,2048]{1,0:T(8,128)(2,1)} %param.9) | copy-start | bytes 786436
  7.5 10.5 %copy-start.10 = (bf16[64,2048]{1,0:T(8,128)(2,1)S(1)}, bf16[64,2048]{1,0:T(8,128)(2,1)}, u32[]{:S(2)}) copy-start(bf16[64,2048]{1,0:T(8,128)(2,1)} %param.6) | copy-start | bytes 786436
  11.4 51.0 %collective-permute-start = (bf16[2,512,2048]{1,2,0:T(8,128)(2,1)}, bf16[2,512,2048]{1,2,0:T(8,128)(2,1)}, u32[]{:S(2)}, u32[]{:S(2)}) collective-permute-start(bf16[2,512,2048]{1,2,0:T(8,128)(2,1)} %pad_maximum_fusion.1), channel_id=1, source_target_pairs={{1,0},{2,1},{3,2},{4,3},{5,4},{6,5},{7,6},{8,7},{9,8},{10,9},{11,1... | collective-permute-start | bytes 12582920 | tf_op jit(solution)/shard_map/ppermute | solution.py:21
  76.4 4.9 %copy-start.2 = (f32[16,2,512,64]{2,3,1,0:T(8,128)}, f32[16,2,512,64]{2,3,1,0:T(8,128)S(1)}, u32[]{:S(2)}) copy-start(f32[16,2,512,64]{2,3,1,0:T(8,128)S(1)} %get-tuple-element.17) | copy-start | bytes 12582916
  76.4 3.1 %copy-start.5 = (bf16[1,512,16,128]{3,1,2,0:T(8,128)(2,1)S(1)}, bf16[1,512,16,128]{3,1,2,0:T(8,128)(2,1)}, u32[]{:S(2)}) copy-start(bf16[1,512,16,128]{3,1,2,0:T(8,128)(2,1)} %copy.84) | copy-start | bytes 6291460
  76.4 3.7 %copy-start.6 = (bf16[1,512,16,128]{3,1,2,0:T(8,128)(2,1)S(1)}, bf16[1,512,16,128]{3,1,2,0:T(8,128)(2,1)}, u32[]{:S(2)}) copy-start(bf16[1,512,16,128]{3,1,2,0:T(8,128)(2,1)} %copy.85) | copy-start | bytes 6291460
  81.9 3.7 %copy-start.3 = (f32[16,2,512,64]{2,3,1,0:T(8,128)S(1)}, f32[16,2,512,64]{2,3,1,0:T(8,128)}, u32[]{:S(2)}) copy-start(f32[16,2,512,64]{2,3,1,0:T(8,128)} %copy-done.2) | copy-start | bytes 12582916
  81.9 4.1 %copy-start.7 = (bf16[1,512,16,128]{3,1,2,0:T(8,128)(2,1)S(1)}, bf16[1,512,16,128]{3,1,2,0:T(8,128)(2,1)}, u32[]{:S(2)}) copy-start(bf16[1,512,16,128]{3,1,2,0:T(8,128)(2,1)} %copy.85) | copy-start | bytes 6291460
  87.9 1.4 copy-start.8
  96.0 8.8 %copy-start.4 = (bf16[1,512,16,128]{3,1,0,2:T(8,128)(2,1)S(1)}, bf16[1,512,16,128]{3,1,0,2:T(8,128)(2,1)}, u32[]{:S(2)}) copy-start(bf16[1,512,16,128]{3,1,0,2:T(8,128)(2,1)} %copy.79) | copy-start | bytes 6291460
  104.8 96.7 %collective-permute-start.1 = (f32[2,512,2048]{2,1,0:T(8,128)}, f32[2,512,2048]{2,1,0:T(8,128)}, u32[]{:S(2)}, u32[]{:S(2)}) collective-permute-start(f32[2,512,2048]{2,1,0:T(8,128)} %copy.93), channel_id=1, source_target_pairs={{31,0},{0,1},{1,2},{2,3},{3,4},{4,5},{5,6},{6,7},{7,8},{8,9},{9,10... | collective-permute-start | bytes 25165832 | tf_op jit(solution)/shard_map/ppermute | solution.py:21
  201.5 9.6 %copy-start.1 = (s32[32,8]{0,1:T(8,128)S(1)}, s32[32,8]{0,1:T(8,128)}, u32[]{:S(2)}) copy-start(s32[32,8]{0,1:T(8,128)} %param.10) | copy-start | bytes 3076
where the time goes:
time: 212 us; the launch traced here: 211 us
  waiting for transfers between devices  121 us (57%)
  local copies, waits for them, and re-layouts  48.9 us (23%)
  other arithmetic  20.7 us (10%)
  matrix products  14.9 us (7%)
  starting transfers between devices  4.65 us (2%)
    ppermute x2, waiting for transfers between devices, passed_along(): return lax.ppermute(block, axis, route)  121 us
    squeeze x2, local copies, waits for them, and re-layouts, per_device(): total = blocks[0] + passed_along(blocks[1], 'seq', 1)  17.5 us
    unnamed x32, local copies, waits for them, and re-layouts  11.3 us
    another operation x2, other arithmetic  8.54 us
    another operation x1, other arithmetic, per_device(): blocks = jnp.stack([dk_win, dv_win], axis=1).reshape(2, 2, pool_rows, width)  6.74 us
    another operation x2, local copies, waits for them, and re-layouts, per_device(): v_win = jnp.stack([values, arrived[1]]).reshape(2, pool_rows, HEADS, HD)  6.34 us
    another operation x2, local copies, waits for them, and re-layouts, per_device(): k_win = jnp.stack([keys, arrived[0]]).reshape(2, pool_rows, HEADS, HD)  6.27 us
    ppermute x2, starting transfers between devices, passed_along(): return lax.ppermute(block, axis, route)  4.65 us
  transfers between devices with their start and end apart: 2, of which 2 were waited for; matrix products, arithmetic and copies ran while one was open for 10% of the time, Pallas kernels for 0%

commit v1 on v0

v1 whole, which is shorter than its diff:
```python
import functools
import math

import jax
import jax.numpy as jnp
from jax import lax
from jax.experimental import pallas as pl
from jax.experimental.pallas import tpu as pltpu
from jax.sharding import PartitionSpec as P

HD = 128
GROUP = 64
NLEN = 128
SLOTS = 8
PAIR = 2 * HD
SCALE = 1.0 / math.sqrt(HD)
TO_LOG2 = SCALE / math.log(2.0)
DEAD = -1e30
WIDE = 512
BF16 = jnp.bfloat16
F32 = jnp.float32
NT = (((1,), (1,)), ((), ()))
NN = (((1,), (0,)), ((), ()))
TN = (((0,), (0,)), ((), ()))


def dot(a, b, dims):
    return lax.dot_general(a, b, dims, preferred_element_type=F32)


def two_heads(x):
    zero = jnp.zeros((GROUP, HD), x.dtype)
    first = jnp.concatenate([x[:, :HD], zero], 1)
    second = jnp.concatenate([zero, x[:, HD:]], 1)
    return jnp.concatenate([first, second], 0)


def own_columns(x):
    return jnp.concatenate([x[:GROUP, :HD], x[GROUP:, HD:]], 1)


def column(row):
    tall = jnp.transpose(jnp.broadcast_to(row, (HD, 2 * GROUP)))
    return jnp.concatenate([tall[:GROUP], tall[GROUP:]], 1)


def live_bias(ids, counts, group, first):
    out = []
    for n in range(4):
        hit = jnp.int32(0)
        for j in range(SLOTS):
            match = (ids[group, j] == first + n) & (j < counts[group])
            hit = hit | match.astype(jnp.int32)
        out.append(jnp.where(hit > 0, F32(0.0), F32(DEAD)))
    return out


def softmax_part(k, qb, bias):
    raw = dot(k, qb, NT)
    s = jnp.concatenate([raw[n * NLEN : (n + 1) * NLEN] * TO_LOG2 + bias[n] for n in range(4)], 0)
    peak = jnp.max(s, axis=0, keepdims=True)
    e = jnp.exp2(s - peak)
    total = jnp.sum(e, axis=0, keepdims=True)
    return (e, peak + jnp.log2(total), total)


def own_forward(ids, counts, q, g, k, v, stats, att, weights, dprob):
    step = pl.program_id(0)
    index = lax.axis_index("seq")
    bias = live_bias(ids, counts, index, index * 4)
    for u in range(WIDE // PAIR):
        c = slice(u * PAIR, (u + 1) * PAIR)
        h = slice(u * HD, (u + 1) * HD)
        vv = v[:, c]
        e, lse, total = softmax_part(k[:, c], two_heads(q[:, c]), bias)
        inv = 1.0 / total
        dp = dot(vv, two_heads(g[:, c]), NT)
        row = step * (WIDE // PAIR) + u
        stats[pl.ds(row, 1), :] = lse
        stats[pl.ds(row + 8, 1), :] = jnp.sum(e * dp, axis=0, keepdims=True) * inv
        att[:, c] = own_columns(dot(e.astype(BF16), vv, TN)) * column(inv)
        weights[:, h] = (e * inv).astype(BF16)
        dprob[:, h] = dp.astype(BF16)


def far_forward(ids, counts, q, k, v, lse_out, att, weights):
    step = pl.program_id(0)
    index = lax.axis_index("seq")
    holders = lax.axis_size("seq")
    group = lax.rem(index + holders - 1, holders)
    bias = live_bias(ids, counts, group, index * 4)
    for u in range(WIDE // PAIR):
        c = slice(u * PAIR, (u + 1) * PAIR)
        h = slice(u * HD, (u + 1) * HD)
        e, lse, total = softmax_part(k[:, c], two_heads(q[:, c]), bias)
        inv = 1.0 / total
        row = step * (WIDE // PAIR) + u
        lse_out[pl.ds(row, 1), :] = lse
        att[:, c] = (own_columns(dot(e.astype(BF16), v[:, c], TN)) * column(inv)).astype(BF16)
        weights[:, h] = (e * inv).astype(BF16)


def merged(lse_a, lse_b):
    top = jnp.maximum(lse_a, lse_b)
    a = jnp.exp2(lse_a - top)
    b = jnp.exp2(lse_b - top)
    inv = 1.0 / (a + b)
    return (a * inv, b * inv)


def far_backward(g, k, v, weights, lse_far, stats_own, dq, prob, dscore):
    step = pl.program_id(0)
    for u in range(WIDE // PAIR):
        c = slice(u * PAIR, (u + 1) * PAIR)
        h = slice(u * HD, (u + 1) * HD)
        row = step * (WIDE // PAIR) + u
        share_own, share_far = merged(stats_own[pl.ds(row, 1), :], lse_far[pl.ds(row, 1), :])
        w = weights[:, h].astype(F32)
        dp = dot(v[:, c], two_heads(g[:, c]), NT)
        delta = share_own * stats_own[pl.ds(row + 8, 1), :] + share_far * jnp.sum(
            w * dp, axis=0, keepdims=True
        )
        p = w * share_far
        ds = (p * (dp - delta)).astype(BF16)
        dq[:, c] = (own_columns(dot(ds, k[:, c], TN)) * SCALE).astype(BF16)
        prob[:, h] = p.astype(BF16)
        dscore[:, h] = ds


def finish(
    q, g, q_far, g_far, k, w_own, dp_own, p_far, ds_far, att_own, att_far, stats, lse_far,
    out, dq, dk, dv,
):
    step = pl.program_id(0)
    for u in range(WIDE // PAIR):
        c = slice(u * PAIR, (u + 1) * PAIR)
        h = slice(u * HD, (u + 1) * HD)
        row = step * (WIDE // PAIR) + u
        share_own, share_far = merged(stats[pl.ds(row, 1), :], lse_far[pl.ds(row, 1), :])
        attended = (
            att_own[:, c] * column(share_own) + att_far[:, c].astype(F32) * column(share_far)
        ).astype(BF16)
        out[:, c] = attended
        gg = g[:, c]
        prod = gg.astype(F32) * attended.astype(F32)
        tall = jnp.concatenate([prod[:, :HD], prod[:, HD:]], 0)
        delta = jnp.sum(jnp.transpose(tall), axis=0, keepdims=True)
        p = w_own[:, h].astype(F32) * share_own
        ds = (p * (dp_own[:, h].astype(F32) - delta)).astype(BF16)
        qb = two_heads(q[:, c])
        dq[:, c] = own_columns(dot(ds, k[:, c], TN)) * SCALE
        p_all = jnp.concatenate([p.astype(BF16), p_far[:, h]], 1)
        ds_all = jnp.concatenate([ds, ds_far[:, h]], 1)
        g_all = jnp.concatenate([two_heads(gg), two_heads(g_far[:, c])], 0)
        q_all = jnp.concatenate([qb, two_heads(q_far[:, c])], 0)
        dv[:, c] = dot(p_all, g_all, NN).astype(BF16)
        dk[:, c] = (dot(ds_all, q_all, NN) * SCALE).astype(BF16)


def passed_along(block, distance):
    count = lax.axis_size("seq")
    route = [((i - distance) % count, i) for i in range(count)]
    return lax.ppermute(block, "seq", route)


def call(body, name, ins, outs, flops):
    def spec(kind, rows):
        if kind == "scalar":
            return pl.BlockSpec(memory_space=pltpu.SMEM)
        if kind == "wide":
            return pl.BlockSpec((rows, WIDE), lambda i: (0, i))
        if kind == "half":
            return pl.BlockSpec((rows, WIDE // 2), lambda i: (0, i))
        return pl.BlockSpec((rows, HD), lambda i: (0, 0))

    width = {"wide": 2048, "half": 1024, "rows": HD}
    shapes = [jax.ShapeDtypeStruct((r, width[kind]), t) for kind, r, t in outs]
    return pl.pallas_call(
        body,
        grid=(2048 // WIDE,),
        in_specs=[spec(kind, x.shape[0]) for kind, x in ins],
        out_specs=[spec(kind, r) for kind, r, t in outs],
        out_shape=shapes,
        compiler_params=pltpu.CompilerParams(vmem_limit_bytes=32 << 20),
        cost_estimate=pl.CostEstimate(
            flops=flops, bytes_accessed=4 << 20, transcendentals=0
        ),
        name=name,
    )(*[x for kind, x in ins])


def per_device(queries, keys, values, cotangent, neighbour_ids, neighbour_counts):
    q_far = passed_along(queries, 1)
    g_far = passed_along(cotangent, 1)
    rows = keys.shape[0]
    ids = ("scalar", neighbour_ids)
    counts = ("scalar", neighbour_counts)
    q, g = ("wide", queries), ("wide", cotangent)
    k, v = ("wide", keys), ("wide", values)
    stats, att_own, w_own, dp_own = call(
        own_forward,
        "own_forward",
        [ids, counts, q, g, k, v],
        [("rows", 16, F32), ("wide", GROUP, F32), ("half", rows, BF16), ("half", rows, BF16)],
        1 << 30,
    )
    stats_in = passed_along(stats, 1)
    lse_far, att_far, w_far = call(
        far_forward,
        "far_forward",
        [ids, counts, ("wide", q_far), k, v],
        [("rows", 8, F32), ("wide", GROUP, BF16), ("half", rows, BF16)],
        1 << 30,
    )
    att_back = passed_along(att_far, -1)
    lse_back = passed_along(lse_far, -1)
    dq_far, p_far, ds_far = call(
        far_backward,
        "far_backward",
        [("wide", g_far), k, v, ("half", w_far), ("rows", lse_far), ("rows", stats_in)],
        [("wide", GROUP, BF16), ("half", rows, BF16), ("half", rows, BF16)],
        1 << 30,
    )
    dq_back = passed_along(dq_far, -1)
    out, dq_own, dk, dv = call(
        finish,
        "finish",
        [
            q, g, ("wide", q_far), ("wide", g_far), k, ("half", w_own), ("half", dp_own),
            ("half", p_far), ("half", ds_far), ("wide", att_own), ("wide", att_back),
            ("rows", stats), ("rows", lse_back),
        ],
        [("wide", GROUP, BF16), ("wide", GROUP, F32), ("wide", rows, BF16), ("wide", rows, BF16)],
        1 << 30,
    )
    query_grad = (dq_own + dq_back.astype(F32)).astype(BF16)
    return (out, query_grad, dk, dv)


def solution(mesh):
    split = P(("pop", "seq"), None)
    return jax.shard_map(
        per_device,
        mesh=mesh,
        in_specs=(split, split, split, split, P("pop", None), P("pop")),
        out_specs=(split, split, split, split),
        check_vma=False,
    )
```

time: 212 us -> 40.3 us (0.19)
  the two profiles are of different devices: /device:TPU:160 before, /device:TPU:1 now
where the time goes in v1:
time: 40.3 us; the launch traced here: 39.7 us
  Pallas kernels  19.9 us (49%)
  starting transfers between devices  9.19 us (23%)
  local copies, waits for them, and re-layouts  6.52 us (16%)
  waiting for transfers between devices  2.57 us (6%)
  other arithmetic  0.77 us (2%)
  between operations  0.72 us (2%)
    pallas_call x4, Pallas kernels, call(): pl.pallas_call(body, grid=(2048 // WIDE,), in_specs=[spec(kind, x.shape[0...  19.9 us
    ppermute x6, starting transfers between devices, passed_along(): return lax.ppermute(block, 'seq', route)  9.19 us
    unnamed x21, local copies, waits for them, and re-layouts  6.52 us
    ppermute x6, waiting for transfers between devices, passed_along(): return lax.ppermute(block, 'seq', route)  2.57 us
  transfers between devices with their start and end apart: 6, of which 1 were waited for; matrix products, arithmetic and copies ran while one was open for 2% of the time, Pallas kernels for 50%

profile of v1, /device:TPU:1, one launch (start us, length us, event | category | flops | bytes accessed | tf_op | source)
XLA Modules:
  0.0 39.7 jit_solution(9416616332698785367)
XLA Ops:
  0.6 2.7 %collective-permute-start = (bf16[64,2048]{1,0:T(8,128)(2,1)}, bf16[64,2048]{1,0:T(8,128)(2,1)S(1)}, u32[]{:S(2)}, u32[]{:S(2)}) collective-permute-start(bf16[64,2048]{1,0:T(8,128)(2,1)} %q.3), channel_id=1, source_target_pairs={{31,0},{0,1},{1,2},{2,3},{3,4},{4,5},{5,6},{6,7},{7,8},{8,9},{9,10... | collective-permute-start | bytes 786440 | tf_op jit(solution)/shard_map/ppermute | solution.py:163
  3.3 0.1 collective-permute-start.1
  3.4 0.8 %copy.10.ids = s32[32,8]{1,0:T(8,128)S(1)} copy(s32[32,8]{0,1:T(8,128)} %param.10) | data formatting | bytes 2048 | tf_op args[4]
  4.2 0.0 copy-start
  4.2 1.6 %copy-done = bf16[512,2048]{1,0:T(8,128)(2,1)S(1)} copy-done((bf16[512,2048]{1,0:T(8,128)(2,1)S(1)}, bf16[512,2048]{1,0:T(8,128)(2,1)}, u32[]{:S(2)}) %copy-start) | copy-done | bytes 2097176
  5.8 0.0 copy-start.2
  5.8 1.6 %copy-done.2 = bf16[512,2048]{1,0:T(8,128)(2,1)S(1)} copy-done((bf16[512,2048]{1,0:T(8,128)(2,1)S(1)}, bf16[512,2048]{1,0:T(8,128)(2,1)}, u32[]{:S(2)}) %copy-start.2) | copy-done | bytes 2097176
  7.3 0.9 %copy-done.4 = bf16[64,2048]{1,0:T(8,128)(2,1)S(1)} copy-done((bf16[64,2048]{1,0:T(8,128)(2,1)S(1)}, bf16[64,2048]{1,0:T(8,128)(2,1)}, u32[]{:S(2)}) %copy-start.4) | copy-done | bytes 262168
  8.3 0.9 %copy-done.6 = bf16[64,2048]{1,0:T(8,128)(2,1)S(1)} copy-done((bf16[64,2048]{1,0:T(8,128)(2,1)S(1)}, bf16[64,2048]{1,0:T(8,128)(2,1)}, u32[]{:S(2)}) %copy-start.6) | copy-done | bytes 262168
  9.2 0.7 %copy-done.8 = s32[32]{0:T(128)S(1)} copy-done((s32[32]{0:T(128)S(1)}, s32[32]{0:T(128)}, u32[]{:S(2)}) %copy-start.8) | copy-done | bytes 152
  9.9 4.5 %own_forward.1 = (f32[16,128]{1,0:T(8,128)S(1)}, f32[64,2048]{1,0:T(8,128)S(1)}, bf16[512,1024]{1,0:T(8,128)(2,1)S(1)}, bf16[512,1024]{1,0:T(8,128)(2,1)S(1)}) custom-call(s32[32,8]{1,0:T(8,128)S(1)} %copy.10.ids, s32[32]{0:T(128)S(1)} %copy-done.8, bf16[64,2048]{1,0:T(8,128)(2,1)S(1)} %copy-done.4, bf16[64,2048]{1,0:T(8,128)(2,1)S(1)} %copy-done.6, ...), custom_call_target="tpu_custom_call" | custom-call | flops 1073741824 | bytes 4194304 | tf_op jit(solution)/shard_map/own_forward/pallas_call | solution.py:178
  14.4 1.6 %collective-permute-start.2 = (f32[16,128]{1,0:T(8,128)S(1)}, f32[16,128]{1,0:T(8,128)S(1)}, u32[]{:S(2)}, u32[]{:S(2)}) collective-permute-start(f32[16,128]{1,0:T(8,128)S(1)} %get-tuple-element.22.stats), channel_id=1, source_target_pairs={{31,0},{0,1},{1,2},{2,3},{3,4},{4,5},{5,6},{6,7},{7,8},{8,9},{9,10... | collective-permute-start | bytes 24584 | tf_op jit(solution)/shard_map/ppermute | solution.py:163
  16.0 0.0 collective-permute-done.q.q_far
  16.0 0.0 copy-done.1
  16.0 0.0 copy-done.3
  16.0 0.0 copy-done.9
  16.0 5.1 %far_forward.1 = (f32[8,128]{1,0:T(8,128)S(1)}, bf16[64,2048]{1,0:T(8,128)(2,1)S(1)}, bf16[512,1024]{1,0:T(8,128)(2,1)S(1)}) custom-call(s32[32,8]{1,0:T(8,128)S(1)} %copy.10.ids, s32[32]{0:T(128)S(1)} %copy-done.9, bf16[64,2048]{1,0:T(8,128)(2,1)S(1)} %collective-permute-done.q.q_far, bf16[512,2048]{1,0:T(8,128)(2,1)S(1)} %copy-done.1, ...), custom_call_target="tpu_custom_call" | custom-call | flops 1073741824 | bytes 4194304 | tf_op jit(solution)/shard_map/far_forward/pallas_call | solution.py:178
  21.1 0.1 collective-permute-start.3
  21.2 0.0 collective-permute-done.2.stats_own
  21.2 0.0 collective-permute-done.1.g.g_far
  21.3 0.0 copy-start.5
  21.3 0.0 copy-start.7
  21.3 4.7 %far_backward.1 = (bf16[64,2048]{1,0:T(8,128)(2,1)S(1)}, bf16[512,1024]{1,0:T(8,128)(2,1)S(1)}, bf16[512,1024]{1,0:T(8,128)(2,1)S(1)}) custom-call(bf16[64,2048]{1,0:T(8,128)(2,1)S(1)} %collective-permute-done.1.g.g_far, bf16[512,2048]{1,0:T(8,128)(2,1)S(1)} %copy-done.1, bf16[512,2048]{1,0:T(8,128)(2,1)S(1)} %copy-done.3, ...), custom_call_target="tpu_custom_call" | custom-call | flops 1073741824 | bytes 4194304 | tf_op jit(solution)/shard_map/far_backward/pallas_call | solution.py:178
  26.0 4.3 %collective-permute-start.5 = (bf16[64,2048]{1,0:T(8,128)(2,1)S(1)}, bf16[64,2048]{1,0:T(8,128)(2,1)S(1)}, u32[]{:S(2)}, u32[]{:S(2)}) collective-permute-start(bf16[64,2048]{1,0:T(8,128)(2,1)S(1)} %get-tuple-element.29), channel_id=1, source_target_pairs={{1,0},{2,1},{3,2},{4,3},{5,4},{6,5},{7,6},{8,7},{9,8},{10,9},{11,1... | collective-permute-start | bytes 786440 | tf_op jit(solution)/shard_map/ppermute | solution.py:163
  30.3 0.5 %collective-permute-start.4 = (f32[8,128]{1,0:T(8,128)S(1)}, f32[8,128]{1,0:T(8,128)S(1)}, u32[]{:S(2)}, u32[]{:S(2)}) collective-permute-start(f32[8,128]{1,0:T(8,128)S(1)} %get-tuple-element.21.lse_far), channel_id=1, source_target_pairs={{1,0},{2,1},{3,2},{4,3},{5,4},{6,5},{7,6},{8,7},{9,8},{10,9},{11,1... | collective-permute-start | bytes 12296 | tf_op jit(solution)/shard_map/ppermute | solution.py:163
  30.8 2.6 %collective-permute-done.4.lse_far = f32[8,128]{1,0:T(8,128)S(1)} collective-permute-done((f32[8,128]{1,0:T(8,128)S(1)}, f32[8,128]{1,0:T(8,128)S(1)}, u32[]{:S(2)}, u32[]{:S(2)}) %collective-permute-start.4) | collective-permute-done | bytes 4128 | tf_op jit(solution)/shard_map/ppermute | solution.py:163
  33.3 0.0 collective-permute-done.3.att_far
  33.3 0.0 copy-done.5
  33.3 0.0 copy-done.7
  33.3 5.5 %finish.1 = (bf16[64,2048]{1,0:T(8,128)(2,1)}, f32[64,2048]{1,0:T(8,128)S(1)}, bf16[512,2048]{1,0:T(8,128)(2,1)}, bf16[512,2048]{1,0:T(8,128)(2,1)}) custom-call(bf16[64,2048]{1,0:T(8,128)(2,1)S(1)} %copy-done.5, bf16[64,2048]{1,0:T(8,128)(2,1)S(1)} %copy-done.7, bf16[64,2048]{1,0:T(8,128)(2,1)S(1)} %collective-permute-done.q.q_far, ...), custom_call_target="tpu_custom_call" | custom-call | flops 1073741824 | bytes 4194304 | tf_op jit(solution)/shard_map/finish/pallas_call | solution.py:178
  38.9 0.0 collective-permute-done.5
  38.9 0.8 %add_convert_fusion = bf16[64,2048]{1,0:T(8,128)(2,1)} fusion(f32[64,2048]{1,0:T(8,128)S(1)} %get-tuple-element.28, bf16[64,2048]{1,0:T(8,128)(2,1)S(1)} %collective-permute-done.5), kind=kLoop, calls=%fused_computation | loop fusion | flops 393216 | bytes 1048576 | tf_op jit(solution)/shard_map/convert_element_type | solution.py:236
  (6 shorter events, 0.0 us)
Async XLA Ops:
  0.6 15.3 %collective-permute-start = (bf16[64,2048]{1,0:T(8,128)(2,1)}, bf16[64,2048]{1,0:T(8,128)(2,1)S(1)}, u32[]{:S(2)}, u32[]{:S(2)}) collective-permute-start(bf16[64,2048]{1,0:T(8,128)(2,1)} %q.3), channel_id=1, source_target_pairs={{31,0},{0,1},{1,2},{2,3},{3,4},{4,5},{5,6},{6,7},{7,8},{8,9},{9,10... | collective-permute-start | bytes 786440 | tf_op jit(solution)/shard_map/ppermute | solution.py:163
  3.3 17.9 %collective-permute-start.1 = (bf16[64,2048]{1,0:T(8,128)(2,1)}, bf16[64,2048]{1,0:T(8,128)(2,1)S(1)}, u32[]{:S(2)}, u32[]{:S(2)}) collective-permute-start(bf16[64,2048]{1,0:T(8,128)(2,1)} %g.3), channel_id=1, source_target_pairs={{31,0},{0,1},{1,2},{2,3},{3,4},{4,5},{5,6},{6,7},{7,8},{8,9},{9,10... | collective-permute-start | bytes 786440 | tf_op jit(solution)/shard_map/ppermute | solution.py:163
  4.2 1.6 %copy-start = (bf16[512,2048]{1,0:T(8,128)(2,1)S(1)}, bf16[512,2048]{1,0:T(8,128)(2,1)}, u32[]{:S(2)}) copy-start(bf16[512,2048]{1,0:T(8,128)(2,1)} %k.7) | copy-start | bytes 6291460
  5.8 1.6 %copy-start.2 = (bf16[512,2048]{1,0:T(8,128)(2,1)S(1)}, bf16[512,2048]{1,0:T(8,128)(2,1)}, u32[]{:S(2)}) copy-start(bf16[512,2048]{1,0:T(8,128)(2,1)} %v.5) | copy-start | bytes 6291460
  7.3 0.9 %copy-start.4 = (bf16[64,2048]{1,0:T(8,128)(2,1)S(1)}, bf16[64,2048]{1,0:T(8,128)(2,1)}, u32[]{:S(2)}) copy-start(bf16[64,2048]{1,0:T(8,128)(2,1)} %q.3) | copy-start | bytes 786436
  8.3 0.9 %copy-start.6 = (bf16[64,2048]{1,0:T(8,128)(2,1)S(1)}, bf16[64,2048]{1,0:T(8,128)(2,1)}, u32[]{:S(2)}) copy-start(bf16[64,2048]{1,0:T(8,128)(2,1)} %g.3) | copy-start | bytes 786436
  9.2 0.7 %copy-start.8 = (s32[32]{0:T(128)S(1)}, s32[32]{0:T(128)}, u32[]{:S(2)}) copy-start(s32[32]{0:T(128)} %counts.3) | copy-start | bytes 388
  9.9 6.1 %copy-start.1 = (bf16[512,2048]{1,0:T(8,128)(2,1)S(1)}, bf16[512,2048]{1,0:T(8,128)(2,1)}, u32[]{:S(2)}) copy-start(bf16[512,2048]{1,0:T(8,128)(2,1)} %k.7) | copy-start | bytes 6291460
  9.9 6.1 %copy-start.3 = (bf16[512,2048]{1,0:T(8,128)(2,1)S(1)}, bf16[512,2048]{1,0:T(8,128)(2,1)}, u32[]{:S(2)}) copy-start(bf16[512,2048]{1,0:T(8,128)(2,1)} %v.5) | copy-start | bytes 6291460
  9.9 6.1 %copy-start.9 = (s32[32]{0:T(128)S(1)}, s32[32]{0:T(128)}, u32[]{:S(2)}) copy-start(s32[32]{0:T(128)} %counts.3) | copy-start | bytes 388
  14.4 6.9 %collective-permute-start.2 = (f32[16,128]{1,0:T(8,128)S(1)}, f32[16,128]{1,0:T(8,128)S(1)}, u32[]{:S(2)}, u32[]{:S(2)}) collective-permute-start(f32[16,128]{1,0:T(8,128)S(1)} %get-tuple-element.22.stats), channel_id=1, source_target_pairs={{31,0},{0,1},{1,2},{2,3},{3,4},{4,5},{5,6},{6,7},{7,8},{8,9},{9,10... | collective-permute-start | bytes 24584 | tf_op jit(solution)/shard_map/ppermute | solution.py:163
  21.1 12.2 %collective-permute-start.3 = (bf16[64,2048]{1,0:T(8,128)(2,1)S(1)}, bf16[64,2048]{1,0:T(8,128)(2,1)S(1)}, u32[]{:S(2)}, u32[]{:S(2)}) collective-permute-start(bf16[64,2048]{1,0:T(8,128)(2,1)S(1)} %get-tuple-element.26), channel_id=1, source_target_pairs={{1,0},{2,1},{3,2},{4,3},{5,4},{6,5},{7,6},{8,7},{9,8},{10,9},{11,1... | collective-permute-start | bytes 786440 | tf_op jit(solution)/shard_map/ppermute | solution.py:163
  21.3 12.1 %copy-start.5 = (bf16[64,2048]{1,0:T(8,128)(2,1)S(1)}, bf16[64,2048]{1,0:T(8,128)(2,1)}, u32[]{:S(2)}) copy-start(bf16[64,2048]{1,0:T(8,128)(2,1)} %q.3) | copy-start | bytes 786436
  21.3 12.1 %copy-start.7 = (bf16[64,2048]{1,0:T(8,128)(2,1)S(1)}, bf16[64,2048]{1,0:T(8,128)(2,1)}, u32[]{:S(2)}) copy-start(bf16[64,2048]{1,0:T(8,128)(2,1)} %g.3) | copy-start | bytes 786436
  26.0 12.9 %collective-permute-start.5 = (bf16[64,2048]{1,0:T(8,128)(2,1)S(1)}, bf16[64,2048]{1,0:T(8,128)(2,1)S(1)}, u32[]{:S(2)}, u32[]{:S(2)}) collective-permute-start(bf16[64,2048]{1,0:T(8,128)(2,1)S(1)} %get-tuple-element.29), channel_id=1, source_target_pairs={{1,0},{2,1},{3,2},{4,3},{5,4},{6,5},{7,6},{8,7},{9,8},{10,9},{11,1... | collective-permute-start | bytes 786440 | tf_op jit(solution)/shard_map/ppermute | solution.py:163
  30.3 3.0 %collective-permute-start.4 = (f32[8,128]{1,0:T(8,128)S(1)}, f32[8,128]{1,0:T(8,128)S(1)}, u32[]{:S(2)}, u32[]{:S(2)}) collective-permute-start(f32[8,128]{1,0:T(8,128)S(1)} %get-tuple-element.21.lse_far), channel_id=1, source_target_pairs={{1,0},{2,1},{3,2},{4,3},{5,4},{6,5},{7,6},{8,7},{9,8},{10,9},{11,1... | collective-permute-start | bytes 12296 | tf_op jit(solution)/shard_map/ppermute | solution.py:163

commit v2 on v1

v2 whole, which is shorter than its diff:
```python
import math

import jax
import jax.numpy as jnp
from jax import lax
from jax.experimental import pallas as pl
from jax.experimental.pallas import tpu as pltpu
from jax.sharding import PartitionSpec as P

HD = 128
GROUP = 64
NLEN = 128
SLOTS = 8
HELD = 4
WIDTH = 2048
PAIR = 2 * HD
PAIRS = WIDTH // PAIR
ROWS = HELD * NLEN
SCALE = 1.0 / math.sqrt(HD)
TO_LOG2 = SCALE / math.log(2.0)
DEAD = -1e30
LOADS = (0, 2, 5, 8)
BF16 = jnp.bfloat16
F32 = jnp.float32
NT = (((1,), (1,)), ((), ()))
NN = (((1,), (0,)), ((), ()))
TN = (((0,), (0,)), ((), ()))
VMEM = pl.BlockSpec(memory_space=pltpu.VMEM)
HBM = pl.BlockSpec(memory_space=pltpu.HBM)


def dot(a, b, dims):
    return lax.dot_general(a, b, dims, preferred_element_type=F32)


def wide(p):
    return slice(p * PAIR, (p + 1) * PAIR)


def half(p):
    return slice(p * HD, (p + 1) * HD)


def two_heads(x):
    zero = jnp.zeros((GROUP, HD), x.dtype)
    first = jnp.concatenate([x[:, :HD], zero], 1)
    second = jnp.concatenate([zero, x[:, HD:]], 1)
    return jnp.concatenate([first, second], 0)


def own_columns(x):
    return jnp.concatenate([x[:GROUP, :HD], x[GROUP:, HD:]], 1)


def head_sums(x):
    tall = jnp.concatenate([x[:, :HD], x[:, HD:]], 0)
    return jnp.sum(jnp.transpose(tall), axis=0, keepdims=True)


def as_columns(rows):
    return jnp.transpose(jnp.concatenate([rows, jnp.zeros((HD - PAIRS, HD), F32)], 0))


def spread(columns, p):
    tall = jnp.broadcast_to(columns[:, p : p + 1], (2 * GROUP, HD))
    return jnp.concatenate([tall[:GROUP], tall[GROUP:]], 1)


def live_bias(ids, counts, group, first, n):
    hit = jnp.int32(0)
    for j in range(SLOTS):
        match = (ids[j, group] == first + n) & (j < counts[group])
        hit = hit | match.astype(jnp.int32)
    return jnp.where(hit > 0, F32(0.0), F32(DEAD))


def softmax_part(k, qb, bias):
    raw = dot(k, qb, NT)
    s = jnp.concatenate(
        [raw[n * NLEN : (n + 1) * NLEN] * TO_LOG2 + bias[n] for n in range(HELD)], 0
    )
    peak = jnp.max(s, axis=0, keepdims=True)
    e = jnp.exp2(s - peak)
    return (e.astype(BF16), peak, jnp.sum(e, axis=0, keepdims=True))


def merged(peak_a, total_a, peak_b, total_b):
    top = jnp.maximum(peak_a, peak_b)
    a = jnp.exp2(peak_a - top)
    b = jnp.exp2(peak_b - top)
    inv = 1.0 / (a * total_a + b * total_b)
    return (a * inv, b * inv)


def pieces(x, count):
    out = []
    for _ in range(count - 1):
        out.append(x.astype(BF16).astype(F32))
        x = x - out[-1]
    return out + [x]


def packed(figures):
    tall = []
    for rows, count in figures:
        tall += pieces(jnp.concatenate([rows[:, :GROUP], rows[:, GROUP:]], 0), count)
    tall = jnp.concatenate(tall + [jnp.zeros((HD - 16 * len(tall), GROUP), F32)], 0)
    tall = jnp.concatenate([tall, jnp.zeros((HD, GROUP), F32)], 1)
    return jnp.transpose(tall)[:GROUP].astype(BF16)


def unpacked(block, counts):
    tall = jnp.transpose(jnp.concatenate([block.astype(F32), jnp.zeros((GROUP, HD), F32)], 0))
    out, at = [], 0
    for count in counts:
        x = tall[at : at + 16]
        for n in range(1, count):
            x = x + tall[at + 16 * n : at + 16 * n + 16]
        out.append(jnp.concatenate([x[:PAIRS, :GROUP], x[PAIRS:, :GROUP]], 1))
        at += 16 * count
    return out


def own_forward(
    ids_hbm, counts_hbm, q_hbm, g_hbm, k_hbm, v_hbm,
    stats, numer, weights, dprob, bias_far, q, g, k, v,
    ids, counts, sems,
):
    copies = [
        pltpu.make_async_copy(ids_hbm, ids, sems.at[0]),
        pltpu.make_async_copy(counts_hbm, counts, sems.at[1]),
        pltpu.make_async_copy(q_hbm, q, sems.at[2]),
        pltpu.make_async_copy(g_hbm, g.at[:, :WIDTH], sems.at[3]),
    ]
    for n in range(len(LOADS) - 1):
        c = slice(LOADS[n] * PAIR, LOADS[n + 1] * PAIR)
        copies.append(pltpu.make_async_copy(k_hbm.at[:, c], k.at[:, c], sems.at[4 + 2 * n]))
        copies.append(pltpu.make_async_copy(v_hbm.at[:, c], v.at[:, c], sems.at[5 + 2 * n]))
    for copy in copies:
        copy.start()
    index = lax.axis_index("seq")
    before = lax.rem(index + lax.axis_size("seq") - 1, lax.axis_size("seq"))
    copies[0].wait()
    copies[1].wait()
    bias = [live_bias(ids, counts, index, index * HELD, n) for n in range(HELD)]
    for n in range(HELD):
        bias_far[n : n + 1, :] = jnp.full(
            (1, HD), live_bias(ids, counts, before, index * HELD, n), F32
        )
    bias_far[HELD:, :] = jnp.zeros((8 - HELD, HD), F32)
    copies[2].wait()
    copies[3].wait()
    for p in range(PAIRS):
        c, h = wide(p), half(p)
        if p in LOADS:
            n = LOADS.index(p)
            copies[4 + 2 * n].wait()
            copies[5 + 2 * n].wait()
        gg = g[:, c]
        e, peak, total = softmax_part(k[:, c], two_heads(q[:, c]), bias)
        part = own_columns(dot(e, v[:, c], TN))
        weights[:, h] = e
        numer[:, c] = part
        dprob[:, h] = dot(v[:, c], two_heads(gg), NT).astype(BF16)
        stats[p : p + 1, :] = peak
        stats[8 + p : 9 + p, :] = total
        stats[16 + p : 17 + p, :] = head_sums(part * gg.astype(F32))
    g[:, WIDTH:] = packed([(stats[:8, :], 3), (stats[8:16, :], 2), (stats[16:, :], 2)])


def far_forward(bias_ref, q, k, v, message, weights, stats):
    bias = [bias_ref[n : n + 1, :] for n in range(HELD)]
    for p in range(PAIRS):
        c, h = wide(p), half(p)
        e, peak, total = softmax_part(k[:, c], two_heads(q[:, c]), bias)
        message[:, c] = own_columns(dot(e, v[:, c], TN)).astype(BF16)
        weights[:, h] = e
        stats[p : p + 1, :] = peak
        stats[8 + p : 9 + p, :] = total
    message[:, WIDTH:] = packed([(stats[:8, :], 3), (stats[8:, :], 2)])


def far_backward(g, k, v, weights, message, stats, dq, prob, dscore):
    peak_own, total_own, dot_own = unpacked(g[:, WIDTH:], (3, 2, 2))
    own, far = merged(peak_own, total_own, stats[0:8, :], stats[8:16, :])
    delta_own = own * dot_own
    for p in range(PAIRS):
        c, h = wide(p), half(p)
        gg = g[:, c]
        row = slice(p, p + 1)
        delta = delta_own[row] + far[row] * head_sums(
            message[:, c].astype(F32) * gg.astype(F32)
        )
        dp = dot(v[:, c], two_heads(gg), NT)
        pr = weights[:, h].astype(F32) * far[row]
        ds = (pr * (dp - delta)).astype(BF16)
        dq[:, c] = (own_columns(dot(ds, k[:, c], TN)) * SCALE).astype(BF16)
        prob[:, h] = pr.astype(BF16)
        dscore[:, h] = ds


def finish(
    q, g, q_far, g_far, k, w_own, dp_own, p_far, ds_far, numer, message, stats,
    out_hbm, dq, dk_hbm, dv_hbm,
    out, dk, dv, sems,
):
    peak_far, total_far = unpacked(message[:, WIDTH:], (3, 2))
    own, far = merged(stats[0:8, :], stats[8:16, :], peak_far, total_far)
    own_tall, far_tall = as_columns(own), as_columns(far)
    copies = []
    for p in range(PAIRS):
        c, h = wide(p), half(p)
        row = slice(p, p + 1)
        gg = g[:, c]
        attended = (
            numer[:, c] * spread(own_tall, p) + message[:, c].astype(F32) * spread(far_tall, p)
        ).astype(BF16)
        out[:, c] = attended
        delta = head_sums(gg.astype(F32) * attended.astype(F32))
        pr = w_own[:, h].astype(F32) * own[row]
        ds = (pr * (dp_own[:, h].astype(F32) - delta)).astype(BF16)
        dq[:, c] = own_columns(dot(ds, k[:, c], TN)) * SCALE
        p_all = jnp.concatenate([pr.astype(BF16), p_far[:, h]], 1)
        ds_all = jnp.concatenate([ds, ds_far[:, h]], 1)
        g_all = jnp.concatenate([two_heads(gg), two_heads(g_far[:, c])], 0)
        q_all = jnp.concatenate([two_heads(q[:, c]), two_heads(q_far[:, c])], 0)
        dv[:, c] = dot(p_all, g_all, NN).astype(BF16)
        dk[:, c] = (dot(ds_all, q_all, NN) * SCALE).astype(BF16)
        for kind, (held, to) in enumerate(((out, out_hbm), (dk, dk_hbm), (dv, dv_hbm))):
            copy = pltpu.make_async_copy(held.at[:, c], to.at[:, c], sems.at[3 * p + kind])
            copy.start()
            copies.append(copy)
    for copy in copies:
        copy.wait()


def passed_along(block, distance):
    count = lax.axis_size("seq")
    route = [((i - distance) % count, i) for i in range(count)]
    return lax.ppermute(block, "seq", route)


def call(body, name, ins, outs, scratch=()):
    return pl.pallas_call(
        body,
        in_specs=[place for x, place in ins],
        out_specs=[place for shape, kind, place in outs],
        out_shape=[jax.ShapeDtypeStruct(shape, kind) for shape, kind, place in outs],
        scratch_shapes=scratch,
        compiler_params=pltpu.CompilerParams(vmem_limit_bytes=20 << 20),
        cost_estimate=pl.CostEstimate(
            flops=1 << 30, bytes_accessed=4 << 20, transcendentals=0
        ),
        name=name,
    )(*[x for x, place in ins])


def per_device(queries, keys, values, cotangent, neighbour_ids, neighbour_counts):
    dma = pltpu.SemaphoreType.DMA
    pool, tokens, pairs = (ROWS, WIDTH), (GROUP, WIDTH), (ROWS, WIDTH // 2)
    longer = (GROUP, WIDTH + HD)
    q_far = passed_along(queries, 1)
    ids = jnp.transpose(neighbour_ids)
    stats, numer, w_own, dp_own, bias_far, q, g, k, v = call(
        own_forward,
        "own_forward",
        [
            (pltpu.with_memory_space_constraint(x, pltpu.HBM), HBM)
            for x in (ids, neighbour_counts, queries, cotangent, keys, values)
        ],
        [
            ((24, HD), F32, VMEM), (tokens, F32, VMEM), (pairs, BF16, VMEM), (pairs, BF16, VMEM),
            ((8, HD), F32, VMEM), (tokens, BF16, VMEM), (longer, BF16, VMEM), (pool, BF16, VMEM),
            (pool, BF16, VMEM),
        ],
        [
            pltpu.SMEM(ids.shape, jnp.int32),
            pltpu.SMEM(neighbour_counts.shape, jnp.int32),
            dma((2 + 2 * len(LOADS),)),
        ],
    )
    g_far = passed_along(g, 1)
    message, w_far, stats_far = call(
        far_forward,
        "far_forward",
        [(x, VMEM) for x in (bias_far, q_far, k, v)],
        [(longer, BF16, VMEM), (pairs, BF16, VMEM), ((16, HD), F32, VMEM)],
    )
    message_back = passed_along(message, -1)
    dq_far, p_far, ds_far = call(
        far_backward,
        "far_backward",
        [(x, VMEM) for x in (g_far, k, v, w_far, message, stats_far)],
        [(tokens, BF16, VMEM), (pairs, BF16, VMEM), (pairs, BF16, VMEM)],
    )
    dq_back = passed_along(dq_far, -1)
    out, dq_own, dk, dv = call(
        finish,
        "finish",
        [
            (x, VMEM)
            for x in (
                q, g, q_far, g_far, k, w_own, dp_own, p_far, ds_far, numer, message_back, stats
            )
        ],
        [(tokens, BF16, HBM), (tokens, F32, VMEM), (pool, BF16, HBM), (pool, BF16, HBM)],
        [
            pltpu.VMEM(tokens, BF16), pltpu.VMEM(pool, BF16), pltpu.VMEM(pool, BF16),
            dma((3 * PAIRS,)),
        ],
    )
    query_grad = (dq_own + dq_back.astype(F32)).astype(BF16)
    return (out, query_grad, dk, dv)


def solution(mesh):
    split = P(("pop", "seq"), None)
    return jax.shard_map(
        per_device,
        mesh=mesh,
        in_specs=(split, split, split, split, P("pop", None), P("pop")),
        out_specs=(split, split, split, split),
        check_vma=False,
    )
```

time: 40.3 us -> 26.6 us (0.66); the launches traced: 39.7 us -> 26.5 us
  local copies, waits for them, and re-layouts: 6.52 us -> 0 us
  Pallas kernels: 19.9 us -> 15.4 us
  waiting for transfers between devices: 2.57 us -> 0.15 us
    unnamed x21 -> x0, local copies, waits for them, and re-layouts: 6.52 us -> none
    pallas_call x4, Pallas kernels: 19.9 us -> 15.4 us  [call(): pl.pallas_call(body, in_specs=[place for x, place in ins], out_specs=[pla...]
    ppermute x6 -> x4, waiting for transfers between devices: 2.57 us -> 0.15 us  [passed_along(): return lax.ppermute(block, 'seq', route)]
    ppermute x6 -> x4, starting transfers between devices: 9.19 us -> 9.56 us  [passed_along(): return lax.ppermute(block, 'seq', route)]
  transfers between devices with their start and end apart: 6 -> 4, of which waited for: 1 -> 1; matrix products, arithmetic and copies ran while one was open for 2% -> 0% of each run, Pallas kernels for 50% -> 58%
where the time goes in v2:
time: 26.6 us; the launch traced here: 26.5 us
  Pallas kernels  15.4 us (58%)
  starting transfers between devices  9.56 us (36%)
  other arithmetic  0.77 us (3%)
  between operations  0.67 us (3%)
    pallas_call x4, Pallas kernels, call(): pl.pallas_call(body, in_specs=[place for x, place in ins], out_specs=[pla...  15.4 us
    ppermute x4, starting transfers between devices, passed_along(): return lax.ppermute(block, 'seq', route)  9.56 us
    convert_element_type x1, other arithmetic, per_device(): query_grad = (dq_own + dq_back.astype(F32)).astype(BF16)  0.77 us
  transfers between devices with their start and end apart: 4, of which 1 were waited for; matrix products, arithmetic and copies ran while one was open for 0% of the time, Pallas kernels for 58%

profile of v2, /device:TPU:1, one launch (start us, length us, event | category | flops | bytes accessed | tf_op | source)
XLA Modules:
  0.0 26.5 jit_solution(14764448598336941961)
XLA Ops:
  0.6 2.7 %collective-permute-start = (bf16[64,2048]{1,0:T(8,128)(2,1)}, bf16[64,2048]{1,0:T(8,128)(2,1)S(1)}, u32[]{:S(2)}, u32[]{:S(2)}) collective-permute-start(bf16[64,2048]{1,0:T(8,128)(2,1)} %q_hbm.1), channel_id=1, source_target_pairs={{31,0},{0,1},{1,2},{2,3},{3,4},{4,5},{5,6},{6,7},{7,8},{8,9},{9,10... | collective-permute-start | bytes 786440 | tf_op jit(solution)/shard_map/ppermute | solution.py:240
  3.3 5.3 %own_forward.1 = (f32[24,128]{1,0:T(8,128)S(1)}, f32[64,2048]{1,0:T(8,128)S(1)}, bf16[512,1024]{1,0:T(8,128)(2,1)S(1)}, bf16[512,1024]{1,0:T(8,128)(2,1)S(1)}, f...) custom-call(s32[8,32]{1,0:T(8,128)} %bitcast.1, ...), custom_call_target="tpu_custom_call" | custom-call | flops 1073741824 | bytes 4194304 | tf_op jit(solution)/shard_map/own_forward/pallas_call | solution.py:244
  8.6 0.1 collective-permute-start.1
  8.7 0.0 collective-permute-done.q.q_far
  8.7 3.4 %far_forward.1 = (bf16[64,2176]{1,0:T(8,128)(2,1)S(1)}, bf16[512,1024]{1,0:T(8,128)(2,1)S(1)}, f32[16,128]{1,0:T(8,128)S(1)}) custom-call(f32[8,128]{1,0:T(8,128)S(1)} %get-tuple-element.29.bias_ref, bf16[64,2048]{1,0:T(8,128)(2,1)S(1)} %collective-permute-done.q.q_far, bf16[512,2048]{1,0:T(8,128)(2,1)S(1)} %get-tuple-element.25.k, ...), custom_call_target="tpu_custom_call" | custom-call | flops 1073741824 | bytes 4194304 | tf_op jit(solution)/shard_map/far_forward/pallas_call | solution.py:244
  12.1 4.6 %collective-permute-start.2 = (bf16[64,2176]{1,0:T(8,128)(2,1)S(1)}, bf16[64,2176]{1,0:T(8,128)(2,1)S(1)}, u32[]{:S(2)}, u32[]{:S(2)}) collective-permute-start(bf16[64,2176]{1,0:T(8,128)(2,1)S(1)} %get-tuple-element.31.message), channel_id=1, source_target_pairs={{1,0},{2,1},{3,2},{4,3},{5,4},{6,5},{7,6},{8,7},{9,8},{10,9},{11,1... | collective-permute-start | bytes 835592 | tf_op jit(solution)/shard_map/ppermute | solution.py:240
  16.7 0.0 collective-permute-done.1.g.g_far
  16.8 2.9 %far_backward.1 = (bf16[64,2048]{1,0:T(8,128)(2,1)S(1)}, bf16[512,1024]{1,0:T(8,128)(2,1)S(1)}, bf16[512,1024]{1,0:T(8,128)(2,1)S(1)}) custom-call(bf16[64,2176]{1,0:T(8,128)(2,1)S(1)} %collective-permute-done.1.g.g_far, bf16[512,2048]{1,0:T(8,128)(2,1)S(1)} %get-tuple-element.25.k, bf16[512,2048]{1,0:T(8,128)(2,1)S(1)} %get-tuple-element.28.v, ...), custom_call_target="tpu_custom_call" | custom-call | flops 1073741824 | bytes 4194304 | tf_op jit(solution)/shard_map/far_backward/pallas_call | solution.py:244
  19.7 2.2 %collective-permute-start.3 = (bf16[64,2048]{1,0:T(8,128)(2,1)S(1)}, bf16[64,2048]{1,0:T(8,128)(2,1)S(1)}, u32[]{:S(2)}, u32[]{:S(2)}) collective-permute-start(bf16[64,2048]{1,0:T(8,128)(2,1)S(1)} %get-tuple-element.39), channel_id=1, source_target_pairs={{1,0},{2,1},{3,2},{4,3},{5,4},{6,5},{7,6},{8,7},{9,8},{10,9},{11,1... | collective-permute-start | bytes 786440 | tf_op jit(solution)/shard_map/ppermute | solution.py:240
  21.9 0.0 collective-permute-done.2.message
  21.9 3.7 %finish.1 = (bf16[64,2048]{1,0:T(8,128)(2,1)}, f32[64,2048]{1,0:T(8,128)S(1)}, bf16[512,2048]{1,0:T(8,128)(2,1)}, bf16[512,2048]{1,0:T(8,128)(2,1)}) custom-call(bf16[64,2048]{1,0:T(8,128)(2,1)S(1)} %get-tuple-element.23.q, bf16[64,2176]{1,0:T(8,128)(2,1)S(1)} %get-tuple-element.24.g, bf16[64,2048]{1,0:T(8,128)(2,1)S(1)} %collective-permute-done.q.q_far, ...), custom_call_target="tpu_custom_call" | custom-call | flops 1073741824 | bytes 4194304 | tf_op jit(solution)/shard_map/finish/pallas_call | solution.py:244
  25.6 0.1 collective-permute-done.3
  25.7 0.8 %add_convert_fusion = bf16[64,2048]{1,0:T(8,128)(2,1)} fusion(f32[64,2048]{1,0:T(8,128)S(1)} %get-tuple-element.38, bf16[64,2048]{1,0:T(8,128)(2,1)S(1)} %collective-permute-done.3), kind=kLoop, calls=%fused_computation | loop fusion | flops 393216 | bytes 1048576 | tf_op jit(solution)/shard_map/convert_element_type | solution.py:312
Async XLA Ops:
  0.6 8.1 %collective-permute-start = (bf16[64,2048]{1,0:T(8,128)(2,1)}, bf16[64,2048]{1,0:T(8,128)(2,1)S(1)}, u32[]{:S(2)}, u32[]{:S(2)}) collective-permute-start(bf16[64,2048]{1,0:T(8,128)(2,1)} %q_hbm.1), channel_id=1, source_target_pairs={{31,0},{0,1},{1,2},{2,3},{3,4},{4,5},{5,6},{6,7},{7,8},{8,9},{9,10... | collective-permute-start | bytes 786440 | tf_op jit(solution)/shard_map/ppermute | solution.py:240
  8.6 8.1 %collective-permute-start.1 = (bf16[64,2176]{1,0:T(8,128)(2,1)S(1)}, bf16[64,2176]{1,0:T(8,128)(2,1)S(1)}, u32[]{:S(2)}, u32[]{:S(2)}) collective-permute-start(bf16[64,2176]{1,0:T(8,128)(2,1)S(1)} %get-tuple-element.24.g), channel_id=1, source_target_pairs={{31,0},{0,1},{1,2},{2,3},{3,4},{4,5},{5,6},{6,7},{7,8},{8,9},{9,10... | collective-permute-start | bytes 835592 | tf_op jit(solution)/shard_map/ppermute | solution.py:240
  12.1 9.7 %collective-permute-start.2 = (bf16[64,2176]{1,0:T(8,128)(2,1)S(1)}, bf16[64,2176]{1,0:T(8,128)(2,1)S(1)}, u32[]{:S(2)}, u32[]{:S(2)}) collective-permute-start(bf16[64,2176]{1,0:T(8,128)(2,1)S(1)} %get-tuple-element.31.message), channel_id=1, source_target_pairs={{1,0},{2,1},{3,2},{4,3},{5,4},{6,5},{7,6},{8,7},{9,8},{10,9},{11,1... | collective-permute-start | bytes 835592 | tf_op jit(solution)/shard_map/ppermute | solution.py:240
  19.7 6.1 %collective-permute-start.3 = (bf16[64,2048]{1,0:T(8,128)(2,1)S(1)}, bf16[64,2048]{1,0:T(8,128)(2,1)S(1)}, u32[]{:S(2)}, u32[]{:S(2)}) collective-permute-start(bf16[64,2048]{1,0:T(8,128)(2,1)S(1)} %get-tuple-element.39), channel_id=1, source_target_pairs={{1,0},{2,1},{3,2},{4,3},{5,4},{6,5},{7,6},{8,7},{9,8},{10,9},{11,1... | collective-permute-start | bytes 786440 | tf_op jit(solution)/shard_map/ppermute | solution.py:240

commit v3 on v2

--- a/solution.py
+++ b/solution.py
@@ -74,14 +74,30 @@
     return jnp.where(hit > 0, F32(0.0), F32(DEAD))
 
 
-def softmax_part(k, qb, bias):
-    raw = dot(k, qb, NT)
-    s = jnp.concatenate(
-        [raw[n * NLEN : (n + 1) * NLEN] * TO_LOG2 + bias[n] for n in range(HELD)], 0
-    )
-    peak = jnp.max(s, axis=0, keepdims=True)
-    e = jnp.exp2(s - peak)
-    return (e.astype(BF16), peak, jnp.sum(e, axis=0, keepdims=True))
+def score_blocks(a, b):
+    return [dot(a[n * NLEN : (n + 1) * NLEN], b, NT) for n in range(HELD)]
+
+
+def softmax_part(raw, bias):
+    peaks = [
+        jnp.max(raw[n], axis=0, keepdims=True) * TO_LOG2 + bias[n] for n in range(HELD)
+    ]
+    peak = jnp.maximum(jnp.maximum(peaks[0], peaks[1]), jnp.maximum(peaks[2], peaks[3]))
+    e = [
+        jnp.exp2(raw[n] * TO_LOG2 - jnp.where(bias[n] < 0.0, F32(-DEAD), peak))
+        for n in range(HELD)
+    ]
+    sums = [jnp.sum(x, axis=0, keepdims=True) for x in e]
+    return ([x.astype(BF16) for x in e], peak, (sums[0] + sums[1]) + (sums[2] + sums[3]))
+
+
+def staggered(stages):
+    held = {}
+    for t in range(PAIRS + len(stages) - 1):
+        for lag, stage in enumerate(stages):
+            p = t - lag
+            if 0 <= p < PAIRS:
+                held[p] = stage(p, held.get(p))
 
 
 def merged(peak_a, total_a, peak_b, total_b):
@@ -121,9 +137,13 @@
     return out
 
 
+def rows_of(n):
+    return slice(n * NLEN, (n + 1) * NLEN)
+
+
 def own_forward(
     ids_hbm, counts_hbm, q_hbm, g_hbm, k_hbm, v_hbm,
-    stats, numer, weights, dprob, bias_far, q, g, k, v,
+    stats, numer, weights, q, g, k, v,
     ids, counts, sems,
 ):
     copies = [
@@ -139,44 +159,82 @@
     for copy in copies:
         copy.start()
     index = lax.axis_index("seq")
-    before = lax.rem(index + lax.axis_size("seq") - 1, lax.axis_size("seq"))
     copies[0].wait()
     copies[1].wait()
     bias = [live_bias(ids, counts, index, index * HELD, n) for n in range(HELD)]
+    copies[2].wait()
+    copies[3].wait()
+
+    def scores(p, _):
+        if p in LOADS:
+            n = LOADS.index(p)
+            copies[4 + 2 * n].wait()
+            copies[5 + 2 * n].wait()
+        return score_blocks(k[:, wide(p)], two_heads(q[:, wide(p)]))
+
+    def softmax(p, raw):
+        e, peak, total = softmax_part(raw, bias)
+        for n in range(HELD):
+            weights[rows_of(n), half(p)] = e[n]
+        stats[p : p + 1, :] = peak
+        stats[8 + p : 9 + p, :] = total
+        return e
+
+    def sums(p, e):
+        c = wide(p)
+        part = own_columns(dot(jnp.concatenate(e, 0), v[:, c], TN))
+        numer[:, c] = part
+        return part
+
+    def dots(p, part):
+        stats[16 + p : 17 + p, :] = head_sums(part * g[:, wide(p)].astype(F32))
+
+    staggered([scores, softmax, sums, dots])
+    g[:, WIDTH:] = packed([(stats[:8, :], 3), (stats[8:16, :], 2), (stats[16:, :], 2)])
+
+
+def own_dprob(ids_hbm, counts_hbm, g, v, dprob, bias_far, ids, counts, sems):
+    copies = [
+        pltpu.make_async_copy(ids_hbm, ids, sems.at[0]),
+        pltpu.make_async_copy(counts_hbm, counts, sems.at[1]),
+    ]
+    for copy in copies:
+        copy.start()
+    for p in range(PAIRS):
+        c, h = wide(p), half(p)
+        blocks = score_blocks(v[:, c], two_heads(g[:, c]))
+        for n in range(HELD):
+            dprob[rows_of(n), h] = blocks[n].astype(BF16)
+    for copy in copies:
+        copy.wait()
+    index = lax.axis_index("seq")
+    before = lax.rem(index + lax.axis_size("seq") - 1, lax.axis_size("seq"))
     for n in range(HELD):
         bias_far[n : n + 1, :] = jnp.full(
             (1, HD), live_bias(ids, counts, before, index * HELD, n), F32
         )
     bias_far[HELD:, :] = jnp.zeros((8 - HELD, HD), F32)
-    copies[2].wait()
-    copies[3].wait()
-    for p in range(PAIRS):
-        c, h = wide(p), half(p)
-        if p in LOADS:
-            n = LOADS.index(p)
-            copies[4 + 2 * n].wait()
-            copies[5 + 2 * n].wait()
-        gg = g[:, c]
-        e, peak, total = softmax_part(k[:, c], two_heads(q[:, c]), bias)
-        part = own_columns(dot(e, v[:, c], TN))
-        weights[:, h] = e
-        numer[:, c] = part
-        dprob[:, h] = dot(v[:, c], two_heads(gg), NT).astype(BF16)
+
+
+def far_forward(bias_ref, q, k, v, message, weights, stats):
+    bias = [bias_ref[n : n + 1, :] for n in range(HELD)]
+
+    def scores(p, _):
+        return score_blocks(k[:, wide(p)], two_heads(q[:, wide(p)]))
+
+    def softmax(p, raw):
+        e, peak, total = softmax_part(raw, bias)
+        for n in range(HELD):
+            weights[rows_of(n), half(p)] = e[n]
         stats[p : p + 1, :] = peak
         stats[8 + p : 9 + p, :] = total
-        stats[16 + p : 17 + p, :] = head_sums(part * gg.astype(F32))
-    g[:, WIDTH:] = packed([(stats[:8, :], 3), (stats[8:16, :], 2), (stats[16:, :], 2)])
-
-
-def far_forward(bias_ref, q, k, v, message, weights, stats):
-    bias = [bias_ref[n : n + 1, :] for n in range(HELD)]
-    for p in range(PAIRS):
-        c, h = wide(p), half(p)
-        e, peak, total = softmax_part(k[:, c], two_heads(q[:, c]), bias)
-        message[:, c] = own_columns(dot(e, v[:, c], TN)).astype(BF16)
-        weights[:, h] = e
-        stats[p : p + 1, :] = peak
-        stats[8 + p : 9 + p, :] = total
+        return e
+
+    def sums(p, e):
+        part = dot(jnp.concatenate(e, 0), v[:, wide(p)], TN)
+        message[:, wide(p)] = own_columns(part).astype(BF16)
+
+    staggered([scores, softmax, sums])
     message[:, WIDTH:] = packed([(stats[:8, :], 3), (stats[8:, :], 2)])
 
 
@@ -184,19 +242,29 @@
     peak_own, total_own, dot_own = unpacked(g[:, WIDTH:], (3, 2, 2))
     own, far = merged(peak_own, total_own, stats[0:8, :], stats[8:16, :])
     delta_own = own * dot_own
-    for p in range(PAIRS):
-        c, h = wide(p), half(p)
-        gg = g[:, c]
-        row = slice(p, p + 1)
-        delta = delta_own[row] + far[row] * head_sums(
-            message[:, c].astype(F32) * gg.astype(F32)
-        )
-        dp = dot(v[:, c], two_heads(gg), NT)
-        pr = weights[:, h].astype(F32) * far[row]
-        ds = (pr * (dp - delta)).astype(BF16)
-        dq[:, c] = (own_columns(dot(ds, k[:, c], TN)) * SCALE).astype(BF16)
-        prob[:, h] = pr.astype(BF16)
-        dscore[:, h] = ds
+
+    def dprobs(p, _):
+        gg = g[:, wide(p)]
+        dots = head_sums(message[:, wide(p)].astype(F32) * gg.astype(F32))
+        delta = delta_own[p : p + 1] + far[p : p + 1] * dots
+        return (score_blocks(v[:, wide(p)], two_heads(gg)), delta)
+
+    def dscores(p, held):
+        dp, delta = held
+        out = []
+        for n in range(HELD):
+            r, h = rows_of(n), half(p)
+            pr = weights[r, h].astype(F32) * far[p : p + 1]
+            out.append((pr * (dp[n] - delta)).astype(BF16))
+            prob[r, h] = pr.astype(BF16)
+            dscore[r, h] = out[n]
+        return out
+
+    def dqueries(p, ds):
+        part = own_columns(dot(jnp.concatenate(ds, 0), k[:, wide(p)], TN))
+        dq[:, wide(p)] = (part * SCALE).astype(BF16)
+
+    staggered([dprobs, dscores, dqueries])
 
 
 def finish(
@@ -261,25 +329,29 @@
     longer = (GROUP, WIDTH + HD)
     q_far = passed_along(queries, 1)
     ids = jnp.transpose(neighbour_ids)
-    stats, numer, w_own, dp_own, bias_far, q, g, k, v = call(
+    in_hbm = [
+        (pltpu.with_memory_space_constraint(x, pltpu.HBM), HBM)
+        for x in (ids, neighbour_counts, queries, cotangent, keys, values)
+    ]
+    tables = [pltpu.SMEM(ids.shape, jnp.int32), pltpu.SMEM(neighbour_counts.shape, jnp.int32)]
+    stats, numer, w_own, q, g, k, v = call(
         own_forward,
         "own_forward",
+        in_hbm,
         [
-            (pltpu.with_memory_space_constraint(x, pltpu.HBM), HBM)
-            for x in (ids, neighbour_counts, queries, cotangent, keys, values)
+            ((24, HD), F32, VMEM), (tokens, F32, VMEM), (pairs, BF16, VMEM),
+            (tokens, BF16, VMEM), (longer, BF16, VMEM), (pool, BF16, VMEM), (pool, BF16, VMEM),
         ],
-        [
-            ((24, HD), F32, VMEM), (tokens, F32, VMEM), (pairs, BF16, VMEM), (pairs, BF16, VMEM),
-            ((8, HD), F32, VMEM), (tokens, BF16, VMEM), (longer, BF16, VMEM), (pool, BF16, VMEM),
-            (pool, BF16, VMEM),
-        ],
-        [
-            pltpu.SMEM(ids.shape, jnp.int32),
-            pltpu.SMEM(neighbour_counts.shape, jnp.int32),
-            dma((2 + 2 * len(LOADS),)),
-        ],
+        tables + [dma((2 + 2 * len(LOADS),))],
     )
     g_far = passed_along(g, 1)
+    dp_own, bias_far = call(
+        own_dprob,
+        "own_dprob",
+        in_hbm[:2] + [(g, VMEM), (v, VMEM)],
+        [(pairs, BF16, VMEM), ((8, HD), F32, VMEM)],
+        tables + [dma((2,))],
+    )
     message, w_far, stats_far = call(
         far_forward,
         "far_forward",

time: 26.6 us -> 23.8 us (0.89)
  Pallas kernels: 15.4 us -> 11.7 us
  starting transfers between devices: 9.56 us -> 10.5 us
    pallas_call x4 -> x5, Pallas kernels: 15.4 us -> 11.7 us  [call(): pl.pallas_call(body, in_specs=[place for x, place in ins], out_specs=[pla...]
    ppermute x4, starting transfers between devices: 9.56 us -> 10.5 us  [passed_along(): return lax.ppermute(block, 'seq', route)]
  transfers between devices with their start and end apart: 4 -> 4, of which waited for: 1 -> 0; matrix products, arithmetic and copies ran while one was open for 0% -> 0% of each run, Pallas kernels for 58% -> 49%
where the time goes in v3:
time: 23.8 us; the launch traced here: 23.7 us
  Pallas kernels  11.7 us (49%)
  starting transfers between devices  10.5 us (44%)
  other arithmetic  0.76 us (3%)
  between operations  0.69 us (3%)
    pallas_call x5, Pallas kernels, call(): pl.pallas_call(body, in_specs=[place for x, place in ins], out_specs=[pla...  11.7 us
    ppermute x4, starting transfers between devices, passed_along(): return lax.ppermute(block, 'seq', route)  10.5 us
    convert_element_type x1, other arithmetic, per_device(): query_grad = (dq_own + dq_back.astype(F32)).astype(BF16)  0.76 us
  transfers between devices with their start and end apart: 4, of which 0 were waited for; matrix products, arithmetic and copies ran while one was open for 0% of the time, Pallas kernels for 49%

profile of v3, /device:TPU:1, one launch (start us, length us, event | category | flops | bytes accessed | tf_op | source)
XLA Modules:
  0.0 23.7 jit_solution(16206778892574485734)
XLA Ops:
  0.6 2.7 %collective-permute-start = (bf16[64,2048]{1,0:T(8,128)(2,1)}, bf16[64,2048]{1,0:T(8,128)(2,1)S(1)}, u32[]{:S(2)}, u32[]{:S(2)}) collective-permute-start(bf16[64,2048]{1,0:T(8,128)(2,1)} %q_hbm.1), channel_id=1, source_target_pairs={{31,0},{0,1},{1,2},{2,3},{3,4},{4,5},{5,6},{6,7},{7,8},{8,9},{9,10... | collective-permute-start | bytes 786440 | tf_op jit(solution)/shard_map/ppermute | solution.py:308
  3.3 3.6 %own_forward.1 = (f32[24,128]{1,0:T(8,128)S(1)}, f32[64,2048]{1,0:T(8,128)S(1)}, bf16[512,1024]{1,0:T(8,128)(2,1)S(1)}, bf16[64,2048]{1,0:T(8,128)(2,1)S(1)}, bf...) custom-call(s32[8,32]{1,0:T(8,128)} %bitcast.1, s32[32]{0:T(128)} %counts_hbm.3, ...), custom_call_target="tpu_custom_call" | custom-call | flops 1073741824 | bytes 4194304 | tf_op jit(solution)/shard_map/own_forward/pallas_call | solution.py:312
  6.9 0.1 collective-permute-start.1
  7.0 0.8 %own_dprob.1 = (bf16[512,1024]{1,0:T(8,128)(2,1)S(1)}, f32[8,128]{1,0:T(8,128)S(1)}) custom-call(s32[8,32]{1,0:T(8,128)} %bitcast.2, s32[32]{0:T(128)} %counts_hbm.3, bf16[64,2176]{1,0:T(8,128)(2,1)S(1)} %get-tuple-element.24.g, bf16[512,2048]{1,0:T(8,128)(2,1)S(1)} %get-tuple-element.27.v), custom_call_target="tpu_custom_call" | custom-call | flops 1073741824 | bytes 4194304 | tf_op jit(solution)/shard_map/own_dprob/pallas_call | solution.py:312
  7.8 0.0 collective-permute-done.q.q_far
  7.8 1.4 %far_forward.1 = (bf16[64,2176]{1,0:T(8,128)(2,1)S(1)}, bf16[512,1024]{1,0:T(8,128)(2,1)S(1)}, f32[16,128]{1,0:T(8,128)S(1)}) custom-call(f32[8,128]{1,0:T(8,128)S(1)} %get-tuple-element.29.bias_ref, bf16[64,2048]{1,0:T(8,128)(2,1)S(1)} %collective-permute-done.q.q_far, bf16[512,2048]{1,0:T(8,128)(2,1)S(1)} %get-tuple-element.25.k, ...), custom_call_target="tpu_custom_call" | custom-call | flops 1073741824 | bytes 4194304 | tf_op jit(solution)/shard_map/far_forward/pallas_call | solution.py:312
  9.2 5.6 %collective-permute-start.2 = (bf16[64,2176]{1,0:T(8,128)(2,1)S(1)}, bf16[64,2176]{1,0:T(8,128)(2,1)S(1)}, u32[]{:S(2)}, u32[]{:S(2)}) collective-permute-start(bf16[64,2176]{1,0:T(8,128)(2,1)S(1)} %get-tuple-element.31.message), channel_id=1, source_target_pairs={{1,0},{2,1},{3,2},{4,3},{5,4},{6,5},{7,6},{8,7},{9,8},{10,9},{11,1... | collective-permute-start | bytes 835592 | tf_op jit(solution)/shard_map/ppermute | solution.py:308
  14.8 0.0 collective-permute-done.1.g.g_far
  14.8 2.1 %far_backward.1 = (bf16[64,2048]{1,0:T(8,128)(2,1)S(1)}, bf16[512,1024]{1,0:T(8,128)(2,1)S(1)}, bf16[512,1024]{1,0:T(8,128)(2,1)S(1)}) custom-call(bf16[64,2176]{1,0:T(8,128)(2,1)S(1)} %collective-permute-done.1.g.g_far, bf16[512,2048]{1,0:T(8,128)(2,1)S(1)} %get-tuple-element.25.k, bf16[512,2048]{1,0:T(8,128)(2,1)S(1)} %get-tuple-element.27.v, ...), custom_call_target="tpu_custom_call" | custom-call | flops 1073741824 | bytes 4194304 | tf_op jit(solution)/shard_map/far_backward/pallas_call | solution.py:312
  16.9 2.2 %collective-permute-start.3 = (bf16[64,2048]{1,0:T(8,128)(2,1)S(1)}, bf16[64,2048]{1,0:T(8,128)(2,1)S(1)}, u32[]{:S(2)}, u32[]{:S(2)}) collective-permute-start(bf16[64,2048]{1,0:T(8,128)(2,1)S(1)} %get-tuple-element.39), channel_id=1, source_target_pairs={{1,0},{2,1},{3,2},{4,3},{5,4},{6,5},{7,6},{8,7},{9,8},{10,9},{11,1... | collective-permute-start | bytes 786440 | tf_op jit(solution)/shard_map/ppermute | solution.py:308
  19.1 0.0 collective-permute-done.2.message
  19.1 3.7 %finish.1 = (bf16[64,2048]{1,0:T(8,128)(2,1)}, f32[64,2048]{1,0:T(8,128)S(1)}, bf16[512,2048]{1,0:T(8,128)(2,1)}, bf16[512,2048]{1,0:T(8,128)(2,1)}) custom-call(bf16[64,2048]{1,0:T(8,128)(2,1)S(1)} %get-tuple-element.23.q, bf16[64,2176]{1,0:T(8,128)(2,1)S(1)} %get-tuple-element.24.g, bf16[64,2048]{1,0:T(8,128)(2,1)S(1)} %collective-permute-done.q.q_far, ...), custom_call_target="tpu_custom_call" | custom-call | flops 1073741824 | bytes 4194304 | tf_op jit(solution)/shard_map/finish/pallas_call | solution.py:312
  22.9 0.0 collective-permute-done.3
  22.9 0.8 %add_convert_fusion = bf16[64,2048]{1,0:T(8,128)(2,1)} fusion(f32[64,2048]{1,0:T(8,128)S(1)} %get-tuple-element.38, bf16[64,2048]{1,0:T(8,128)(2,1)S(1)} %collective-permute-done.3), kind=kLoop, calls=%fused_computation | loop fusion | flops 393216 | bytes 1048576 | tf_op jit(solution)/shard_map/convert_element_type | solution.py:384
Async XLA Ops:
  0.6 7.2 %collective-permute-start = (bf16[64,2048]{1,0:T(8,128)(2,1)}, bf16[64,2048]{1,0:T(8,128)(2,1)S(1)}, u32[]{:S(2)}, u32[]{:S(2)}) collective-permute-start(bf16[64,2048]{1,0:T(8,128)(2,1)} %q_hbm.1), channel_id=1, source_target_pairs={{31,0},{0,1},{1,2},{2,3},{3,4},{4,5},{5,6},{6,7},{7,8},{8,9},{9,10... | collective-permute-start | bytes 786440 | tf_op jit(solution)/shard_map/ppermute | solution.py:308
  6.9 7.9 %collective-permute-start.1 = (bf16[64,2176]{1,0:T(8,128)(2,1)S(1)}, bf16[64,2176]{1,0:T(8,128)(2,1)S(1)}, u32[]{:S(2)}, u32[]{:S(2)}) collective-permute-start(bf16[64,2176]{1,0:T(8,128)(2,1)S(1)} %get-tuple-element.24.g), channel_id=1, source_target_pairs={{31,0},{0,1},{1,2},{2,3},{3,4},{4,5},{5,6},{6,7},{7,8},{8,9},{9,10... | collective-permute-start | bytes 835592 | tf_op jit(solution)/shard_map/ppermute | solution.py:308
  9.2 9.9 %collective-permute-start.2 = (bf16[64,2176]{1,0:T(8,128)(2,1)S(1)}, bf16[64,2176]{1,0:T(8,128)(2,1)S(1)}, u32[]{:S(2)}, u32[]{:S(2)}) collective-permute-start(bf16[64,2176]{1,0:T(8,128)(2,1)S(1)} %get-tuple-element.31.message), channel_id=1, source_target_pairs={{1,0},{2,1},{3,2},{4,3},{5,4},{6,5},{7,6},{8,7},{9,8},{10,9},{11,1... | collective-permute-start | bytes 835592 | tf_op jit(solution)/shard_map/ppermute | solution.py:308
  16.9 5.9 %collective-permute-start.3 = (bf16[64,2048]{1,0:T(8,128)(2,1)S(1)}, bf16[64,2048]{1,0:T(8,128)(2,1)S(1)}, u32[]{:S(2)}, u32[]{:S(2)}) collective-permute-start(bf16[64,2048]{1,0:T(8,128)(2,1)S(1)} %get-tuple-element.39), channel_id=1, source_target_pairs={{1,0},{2,1},{3,2},{4,3},{5,4},{6,5},{7,6},{8,7},{9,8},{10,9},{11,1... | collective-permute-start | bytes 786440 | tf_op jit(solution)/shard_map/ppermute | solution.py:308

commit v4 on v3

--- a/solution.py
+++ b/solution.py
@@ -20,6 +20,7 @@
 TO_LOG2 = SCALE / math.log(2.0)
 DEAD = -1e30
 LOADS = (0, 2, 5, 8)
+SENT = PAIRS - 1
 BF16 = jnp.bfloat16
 F32 = jnp.float32
 NT = (((1,), (1,)), ((), ()))
@@ -54,7 +55,9 @@
 
 def head_sums(x):
     tall = jnp.concatenate([x[:, :HD], x[:, HD:]], 0)
-    return jnp.sum(jnp.transpose(tall), axis=0, keepdims=True)
+    high = tall.astype(BF16)
+    low = (tall - high.astype(F32)).astype(BF16)
+    return dot(jnp.ones((16, PAIR), BF16), jnp.concatenate([high, low], 1), NT)[0:1]
 
 
 def as_columns(rows):
@@ -267,37 +270,73 @@
     staggered([dprobs, dscores, dqueries])
 
 
-def finish(
+def gradients(
     q, g, q_far, g_far, k, w_own, dp_own, p_far, ds_far, numer, message, stats,
-    out_hbm, dq, dk_hbm, dv_hbm,
+    out_hbm, dq, dk_hbm, dv_hbm, dk_last, dv_last,
     out, dk, dv, sems,
 ):
     peak_far, total_far = unpacked(message[:, WIDTH:], (3, 2))
     own, far = merged(stats[0:8, :], stats[8:16, :], peak_far, total_far)
     own_tall, far_tall = as_columns(own), as_columns(far)
     copies = []
-    for p in range(PAIRS):
-        c, h = wide(p), half(p)
-        row = slice(p, p + 1)
-        gg = g[:, c]
+
+    def send(x, to):
+        copies.append(pltpu.make_async_copy(x, to, sems.at[len(copies)]))
+        copies[-1].start()
+
+    def merge(p, _):
+        c = wide(p)
         attended = (
             numer[:, c] * spread(own_tall, p) + message[:, c].astype(F32) * spread(far_tall, p)
         ).astype(BF16)
         out[:, c] = attended
-        delta = head_sums(gg.astype(F32) * attended.astype(F32))
-        pr = w_own[:, h].astype(F32) * own[row]
+        if p == PAIRS - 1:
+            send(out, out_hbm)
+        return head_sums(g[:, c].astype(F32) * attended.astype(F32))
+
+    def dscores(p, delta):
+        h = half(p)
+        pr = w_own[:, h].astype(F32) * own[p : p + 1]
         ds = (pr * (dp_own[:, h].astype(F32) - delta)).astype(BF16)
+        return (pr.astype(BF16), ds)
+
+    def sums(p, held):
+        pr, ds = held
+        c, h = wide(p), half(p)
         dq[:, c] = own_columns(dot(ds, k[:, c], TN)) * SCALE
-        p_all = jnp.concatenate([pr.astype(BF16), p_far[:, h]], 1)
+        p_all = jnp.concatenate([pr, p_far[:, h]], 1)
         ds_all = jnp.concatenate([ds, ds_far[:, h]], 1)
-        g_all = jnp.concatenate([two_heads(gg), two_heads(g_far[:, c])], 0)
+        g_all = jnp.concatenate([two_heads(g[:, c]), two_heads(g_far[:, c])], 0)
         q_all = jnp.concatenate([two_heads(q[:, c]), two_heads(q_far[:, c])], 0)
-        dv[:, c] = dot(p_all, g_all, NN).astype(BF16)
-        dk[:, c] = (dot(ds_all, q_all, NN) * SCALE).astype(BF16)
-        for kind, (held, to) in enumerate(((out, out_hbm), (dk, dk_hbm), (dv, dv_hbm))):
-            copy = pltpu.make_async_copy(held.at[:, c], to.at[:, c], sems.at[3 * p + kind])
-            copy.start()
-            copies.append(copy)
+        dv_pair = dot(p_all, g_all, NN).astype(BF16)
+        dk_pair = (dot(ds_all, q_all, NN) * SCALE).astype(BF16)
+        if p < SENT:
+            dv[:, c] = dv_pair
+            dk[:, c] = dk_pair
+            send(dv.at[:, c], dv_hbm.at[:, c])
+            send(dk.at[:, c], dk_hbm.at[:, c])
+        else:
+            dv_last[:, wide(p - SENT)] = dv_pair
+            dk_last[:, wide(p - SENT)] = dk_pair
+
+    staggered([merge, dscores, sums])
+    for copy in copies:
+        copy.wait()
+
+
+def last_copies(
+    dk_in, dv_in, dk_last, dv_last, dq_own, dq_far, dk_hbm, dv_hbm, dq_hbm, dq, sems
+):
+    rest = slice(SENT * PAIR, WIDTH)
+    copies = [
+        pltpu.make_async_copy(dk_last, dk_hbm.at[:, rest], sems.at[0]),
+        pltpu.make_async_copy(dv_last, dv_hbm.at[:, rest], sems.at[1]),
+        pltpu.make_async_copy(dq, dq_hbm, sems.at[2]),
+    ]
+    copies[0].start()
+    copies[1].start()
+    dq[...] = (dq_own[...] + dq_far[...].astype(F32)).astype(BF16)
+    copies[2].start()
     for copy in copies:
         copy.wait()
 
@@ -308,13 +347,14 @@
     return lax.ppermute(block, "seq", route)
 
 
-def call(body, name, ins, outs, scratch=()):
+def call(body, name, ins, outs, scratch=(), aliases=None):
     return pl.pallas_call(
         body,
         in_specs=[place for x, place in ins],
         out_specs=[place for shape, kind, place in outs],
         out_shape=[jax.ShapeDtypeStruct(shape, kind) for shape, kind, place in outs],
         scratch_shapes=scratch,
+        input_output_aliases=aliases or {},
         compiler_params=pltpu.CompilerParams(vmem_limit_bytes=20 << 20),
         cost_estimate=pl.CostEstimate(
             flops=1 << 30, bytes_accessed=4 << 20, transcendentals=0
@@ -366,22 +406,33 @@
         [(tokens, BF16, VMEM), (pairs, BF16, VMEM), (pairs, BF16, VMEM)],
     )
     dq_back = passed_along(dq_far, -1)
-    out, dq_own, dk, dv = call(
-        finish,
-        "finish",
+    rest = (ROWS, WIDTH - SENT * PAIR)
+    out, dq_own, dk, dv, dk_last, dv_last = call(
+        gradients,
+        "gradients",
         [
             (x, VMEM)
             for x in (
                 q, g, q_far, g_far, k, w_own, dp_own, p_far, ds_far, numer, message_back, stats
             )
         ],
-        [(tokens, BF16, HBM), (tokens, F32, VMEM), (pool, BF16, HBM), (pool, BF16, HBM)],
+        [
+            (tokens, BF16, HBM), (tokens, F32, VMEM), (pool, BF16, HBM), (pool, BF16, HBM),
+            (rest, BF16, VMEM), (rest, BF16, VMEM),
+        ],
         [
             pltpu.VMEM(tokens, BF16), pltpu.VMEM(pool, BF16), pltpu.VMEM(pool, BF16),
-            dma((3 * PAIRS,)),
+            dma((1 + 2 * SENT,)),
         ],
     )
-    query_grad = (dq_own + dq_back.astype(F32)).astype(BF16)
+    dk, dv, query_grad = call(
+        last_copies,
+        "last_copies",
+        [(dk, HBM), (dv, HBM)] + [(x, VMEM) for x in (dk_last, dv_last, dq_own, dq_back)],
+        [(pool, BF16, HBM), (pool, BF16, HBM), (tokens, BF16, HBM)],
+        [pltpu.VMEM(tokens, BF16), dma((3,))],
+        {0: 0, 1: 1},
+    )
     return (out, query_grad, dk, dv)
 
 

time: 23.8 us -> 23.2 us (0.975)
  other arithmetic: 0.76 us -> 0 us
    convert_element_type x1 -> x0, other arithmetic: 0.76 us -> none  [per_device(): query_grad = (dq_own + dq_back.astype(F32)).astype(BF16)]
    pallas_call x5 -> x6, Pallas kernels: 11.7 us -> 11.8 us  [call(): pl.pallas_call(body, in_specs=[place for x, place in ins], out_specs=[pla...]
  transfers between devices with their start and end apart: 4 -> 4, of which waited for: 0 -> 1; matrix products, arithmetic and copies ran while one was open for 0% -> 0% of each run, Pallas kernels for 49% -> 47%
where the time goes in v4:
time: 23.2 us; the launch traced here: 23.1 us
  Pallas kernels  11.8 us (51%)
  starting transfers between devices  10.5 us (45%)
  between operations  0.68 us (3%)
    pallas_call x6, Pallas kernels, call(): pl.pallas_call(body, in_specs=[place for x, place in ins], out_specs=[pla...  11.8 us
    ppermute x4, starting transfers between devices, passed_along(): return lax.ppermute(block, 'seq', route)  10.5 us
  transfers between devices with their start and end apart: 4, of which 1 were waited for; matrix products, arithmetic and copies ran while one was open for 0% of the time, Pallas kernels for 47%

profile of v4, /device:TPU:1, one launch (start us, length us, event | category | flops | bytes accessed | tf_op | source)
XLA Modules:
  0.0 23.1 jit_solution(16909129127946564109)
XLA Ops:
  0.6 2.7 %collective-permute-start = (bf16[64,2048]{1,0:T(8,128)(2,1)}, bf16[64,2048]{1,0:T(8,128)(2,1)S(1)}, u32[]{:S(2)}, u32[]{:S(2)}) collective-permute-start(bf16[64,2048]{1,0:T(8,128)(2,1)} %q_hbm.1), channel_id=1, source_target_pairs={{31,0},{0,1},{1,2},{2,3},{3,4},{4,5},{5,6},{6,7},{7,8},{8,9},{9,10... | collective-permute-start | bytes 786440 | tf_op jit(solution)/shard_map/ppermute | solution.py:347
  3.3 3.8 %own_forward.1 = (f32[24,128]{1,0:T(8,128)S(1)}, f32[64,2048]{1,0:T(8,128)S(1)}, bf16[512,1024]{1,0:T(8,128)(2,1)S(1)}, bf16[64,2048]{1,0:T(8,128)(2,1)S(1)}, bf...) custom-call(s32[8,32]{1,0:T(8,128)} %bitcast.1, s32[32]{0:T(128)} %counts_hbm.3, ...), custom_call_target="tpu_custom_call" | custom-call | flops 1073741824 | bytes 4194304 | tf_op jit(solution)/shard_map/own_forward/pallas_call | solution.py:351
  7.1 0.1 collective-permute-start.1
  7.2 0.8 %own_dprob.1 = (bf16[512,1024]{1,0:T(8,128)(2,1)S(1)}, f32[8,128]{1,0:T(8,128)S(1)}) custom-call(s32[8,32]{1,0:T(8,128)} %bitcast.2, s32[32]{0:T(128)} %counts_hbm.3, bf16[64,2176]{1,0:T(8,128)(2,1)S(1)} %get-tuple-element.29.g, bf16[512,2048]{1,0:T(8,128)(2,1)S(1)} %get-tuple-element.32.v), custom_call_target="tpu_custom_call" | custom-call | flops 1073741824 | bytes 4194304 | tf_op jit(solution)/shard_map/own_dprob/pallas_call | solution.py:351
  8.0 0.0 collective-permute-done.q.q_far
  8.0 1.4 %far_forward.1 = (bf16[64,2176]{1,0:T(8,128)(2,1)S(1)}, bf16[512,1024]{1,0:T(8,128)(2,1)S(1)}, f32[16,128]{1,0:T(8,128)S(1)}) custom-call(f32[8,128]{1,0:T(8,128)S(1)} %get-tuple-element.34.bias_ref, bf16[64,2048]{1,0:T(8,128)(2,1)S(1)} %collective-permute-done.q.q_far, bf16[512,2048]{1,0:T(8,128)(2,1)S(1)} %get-tuple-element.30.k, ...), custom_call_target="tpu_custom_call" | custom-call | flops 1073741824 | bytes 4194304 | tf_op jit(solution)/shard_map/far_forward/pallas_call | solution.py:351
  9.5 5.3 %collective-permute-start.2 = (bf16[64,2176]{1,0:T(8,128)(2,1)S(1)}, bf16[64,2176]{1,0:T(8,128)(2,1)S(1)}, u32[]{:S(2)}, u32[]{:S(2)}) collective-permute-start(bf16[64,2176]{1,0:T(8,128)(2,1)S(1)} %get-tuple-element.36.message), channel_id=1, source_target_pairs={{1,0},{2,1},{3,2},{4,3},{5,4},{6,5},{7,6},{8,7},{9,8},{10,9},{11,1... | collective-permute-start | bytes 835592 | tf_op jit(solution)/shard_map/ppermute | solution.py:347
  14.8 0.0 collective-permute-done.1.g.g_far
  14.8 1.5 %far_backward.1 = (bf16[64,2048]{1,0:T(8,128)(2,1)S(1)}, bf16[512,1024]{1,0:T(8,128)(2,1)S(1)}, bf16[512,1024]{1,0:T(8,128)(2,1)S(1)}) custom-call(bf16[64,2176]{1,0:T(8,128)(2,1)S(1)} %collective-permute-done.1.g.g_far, bf16[512,2048]{1,0:T(8,128)(2,1)S(1)} %get-tuple-element.30.k, bf16[512,2048]{1,0:T(8,128)(2,1)S(1)} %get-tuple-element.32.v, ...), custom_call_target="tpu_custom_call" | custom-call | flops 1073741824 | bytes 4194304 | tf_op jit(solution)/shard_map/far_backward/pallas_call | solution.py:351
  16.3 2.4 %collective-permute-start.3 = (bf16[64,2048]{1,0:T(8,128)(2,1)S(1)}, bf16[64,2048]{1,0:T(8,128)(2,1)S(1)}, u32[]{:S(2)}, u32[]{:S(2)}) collective-permute-start(bf16[64,2048]{1,0:T(8,128)(2,1)S(1)} %get-tuple-element.48), channel_id=1, source_target_pairs={{1,0},{2,1},{3,2},{4,3},{5,4},{6,5},{7,6},{8,7},{9,8},{10,9},{11,1... | collective-permute-start | bytes 786440 | tf_op jit(solution)/shard_map/ppermute | solution.py:347
  18.7 0.0 collective-permute-done.2.message
  18.7 3.3 %gradients.1 = (bf16[64,2048]{1,0:T(8,128)(2,1)}, f32[64,2048]{1,0:T(8,128)S(1)}, bf16[512,2048]{1,0:T(8,128)(2,1)}, bf16[512,2048]{1,0:T(8,128)(2,1)}, bf16[512...) custom-call(bf16[64,2048]{1,0:T(8,128)(2,1)S(1)} %get-tuple-element.28.q, bf16[64,2176]{1,0:T(8,128)(2,1)S(1)} %get-tuple-element.29.g, ...), custom_call_target="tpu_custom_call" | custom-call | flops 1073741824 | bytes 4194304 | tf_op jit(solution)/shard_map/gradients/pallas_call | solution.py:351
  22.1 0.1 collective-permute-done.3.dq_far
  22.2 0.9 %last_copies.1 = (bf16[512,2048]{1,0:T(8,128)(2,1)}, bf16[512,2048]{1,0:T(8,128)(2,1)}, bf16[64,2048]{1,0:T(8,128)(2,1)}) custom-call(bf16[512,2048]{1,0:T(8,128)(2,1)} %get-tuple-element.43.dk_in, bf16[512,2048]{1,0:T(8,128)(2,1)} %get-tuple-element.44.dv_in, ...), custom_call_target="tpu_custom_call", output_to_operand_aliasing={{0}: (0, {}), {1}: (1, {})} | custom-call | flops 1073741824 | bytes 4194304 | tf_op jit(solution)/shard_map/last_copies/pallas_call | solution.py:351
Async XLA Ops:
  0.6 7.4 %collective-permute-start = (bf16[64,2048]{1,0:T(8,128)(2,1)}, bf16[64,2048]{1,0:T(8,128)(2,1)S(1)}, u32[]{:S(2)}, u32[]{:S(2)}) collective-permute-start(bf16[64,2048]{1,0:T(8,128)(2,1)} %q_hbm.1), channel_id=1, source_target_pairs={{31,0},{0,1},{1,2},{2,3},{3,4},{4,5},{5,6},{6,7},{7,8},{8,9},{9,10... | collective-permute-start | bytes 786440 | tf_op jit(solution)/shard_map/ppermute | solution.py:347
  7.1 7.7 %collective-permute-start.1 = (bf16[64,2176]{1,0:T(8,128)(2,1)S(1)}, bf16[64,2176]{1,0:T(8,128)(2,1)S(1)}, u32[]{:S(2)}, u32[]{:S(2)}) collective-permute-start(bf16[64,2176]{1,0:T(8,128)(2,1)S(1)} %get-tuple-element.29.g), channel_id=1, source_target_pairs={{31,0},{0,1},{1,2},{2,3},{3,4},{4,5},{5,6},{6,7},{7,8},{8,9},{9,10... | collective-permute-start | bytes 835592 | tf_op jit(solution)/shard_map/ppermute | solution.py:347
  9.5 9.2 %collective-permute-start.2 = (bf16[64,2176]{1,0:T(8,128)(2,1)S(1)}, bf16[64,2176]{1,0:T(8,128)(2,1)S(1)}, u32[]{:S(2)}, u32[]{:S(2)}) collective-permute-start(bf16[64,2176]{1,0:T(8,128)(2,1)S(1)} %get-tuple-element.36.message), channel_id=1, source_target_pairs={{1,0},{2,1},{3,2},{4,3},{5,4},{6,5},{7,6},{8,7},{9,8},{10,9},{11,1... | collective-permute-start | bytes 835592 | tf_op jit(solution)/shard_map/ppermute | solution.py:347
  16.3 5.9 %collective-permute-start.3 = (bf16[64,2048]{1,0:T(8,128)(2,1)S(1)}, bf16[64,2048]{1,0:T(8,128)(2,1)S(1)}, u32[]{:S(2)}, u32[]{:S(2)}) collective-permute-start(bf16[64,2048]{1,0:T(8,128)(2,1)S(1)} %get-tuple-element.48), channel_id=1, source_target_pairs={{1,0},{2,1},{3,2},{4,3},{5,4},{6,5},{7,6},{8,7},{9,8},{10,9},{11,1... | collective-permute-start | bytes 786440 | tf_op jit(solution)/shard_map/ppermute | solution.py:347

commit v5 on v4

--- a/solution.py
+++ b/solution.py
@@ -20,7 +20,6 @@
 TO_LOG2 = SCALE / math.log(2.0)
 DEAD = -1e30
 LOADS = (0, 2, 5, 8)
-SENT = PAIRS - 1
 BF16 = jnp.bfloat16
 F32 = jnp.float32
 NT = (((1,), (1,)), ((), ()))
@@ -60,8 +59,14 @@
     return dot(jnp.ones((16, PAIR), BF16), jnp.concatenate([high, low], 1), NT)[0:1]
 
 
+def head_sums_by_transpose(x):
+    tall = jnp.concatenate([x[:, :HD], x[:, HD:]], 0)
+    return jnp.sum(jnp.transpose(tall), axis=0, keepdims=True)
+
+
 def as_columns(rows):
-    return jnp.transpose(jnp.concatenate([rows, jnp.zeros((HD - PAIRS, HD), F32)], 0))
+    empty = jnp.zeros((HD - PAIRS * len(rows), HD), F32)
+    return jnp.transpose(jnp.concatenate(rows + [empty], 0))
 
 
 def spread(columns, p):
@@ -122,21 +127,20 @@
 def packed(figures):
     tall = []
     for rows, count in figures:
-        tall += pieces(jnp.concatenate([rows[:, :GROUP], rows[:, GROUP:]], 0), count)
-    tall = jnp.concatenate(tall + [jnp.zeros((HD - 16 * len(tall), GROUP), F32)], 0)
-    tall = jnp.concatenate([tall, jnp.zeros((HD, GROUP), F32)], 1)
-    return jnp.transpose(tall)[:GROUP].astype(BF16)
+        tall += pieces(rows, count)
+    tall += [jnp.zeros((PAIRS, HD), F32)] * (GROUP // PAIRS - len(tall))
+    return jnp.concatenate(tall, 0).astype(BF16)
 
 
 def unpacked(block, counts):
-    tall = jnp.transpose(jnp.concatenate([block.astype(F32), jnp.zeros((GROUP, HD), F32)], 0))
+    tall = block.astype(F32)
     out, at = [], 0
     for count in counts:
-        x = tall[at : at + 16]
+        x = tall[at : at + PAIRS]
         for n in range(1, count):
-            x = x + tall[at + 16 * n : at + 16 * n + 16]
-        out.append(jnp.concatenate([x[:PAIRS, :GROUP], x[PAIRS:, :GROUP]], 1))
-        at += 16 * count
+            x = x + tall[at + PAIRS * n : at + PAIRS * (n + 1)]
+        out.append(x)
+        at += PAIRS * count
     return out
 
 
@@ -190,7 +194,7 @@
         return part
 
     def dots(p, part):
-        stats[16 + p : 17 + p, :] = head_sums(part * g[:, wide(p)].astype(F32))
+        stats[16 + p : 17 + p, :] = head_sums_by_transpose(part * g[:, wide(p)].astype(F32))
 
     staggered([scores, softmax, sums, dots])
     g[:, WIDTH:] = packed([(stats[:8, :], 3), (stats[8:16, :], 2), (stats[16:, :], 2)])
@@ -272,12 +276,12 @@
 
 def gradients(
     q, g, q_far, g_far, k, w_own, dp_own, p_far, ds_far, numer, message, stats,
-    out_hbm, dq, dk_hbm, dv_hbm, dk_last, dv_last,
+    out_hbm, dq, dk_hbm, dv_hbm,
     out, dk, dv, sems,
 ):
     peak_far, total_far = unpacked(message[:, WIDTH:], (3, 2))
     own, far = merged(stats[0:8, :], stats[8:16, :], peak_far, total_far)
-    own_tall, far_tall = as_columns(own), as_columns(far)
+    factors = as_columns([own, far])
     copies = []
 
     def send(x, to):
@@ -287,7 +291,8 @@
     def merge(p, _):
         c = wide(p)
         attended = (
-            numer[:, c] * spread(own_tall, p) + message[:, c].astype(F32) * spread(far_tall, p)
+            numer[:, c] * spread(factors, p)
+            + message[:, c].astype(F32) * spread(factors, PAIRS + p)
         ).astype(BF16)
         out[:, c] = attended
         if p == PAIRS - 1:
@@ -310,33 +315,23 @@
         q_all = jnp.concatenate([two_heads(q[:, c]), two_heads(q_far[:, c])], 0)
         dv_pair = dot(p_all, g_all, NN).astype(BF16)
         dk_pair = (dot(ds_all, q_all, NN) * SCALE).astype(BF16)
-        if p < SENT:
-            dv[:, c] = dv_pair
-            dk[:, c] = dk_pair
-            send(dv.at[:, c], dv_hbm.at[:, c])
-            send(dk.at[:, c], dk_hbm.at[:, c])
-        else:
-            dv_last[:, wide(p - SENT)] = dv_pair
-            dk_last[:, wide(p - SENT)] = dk_pair
+        dv[:, c] = dv_pair
+        dk[:, c] = dk_pair
+        send(dv.at[:, c], dv_hbm.at[:, c])
+        send(dk.at[:, c], dk_hbm.at[:, c])
 
     staggered([merge, dscores, sums])
     for copy in copies:
         copy.wait()
 
 
-def last_copies(
-    dk_in, dv_in, dk_last, dv_last, dq_own, dq_far, dk_hbm, dv_hbm, dq_hbm, dq, sems
-):
-    rest = slice(SENT * PAIR, WIDTH)
-    copies = [
-        pltpu.make_async_copy(dk_last, dk_hbm.at[:, rest], sems.at[0]),
-        pltpu.make_async_copy(dv_last, dv_hbm.at[:, rest], sems.at[1]),
-        pltpu.make_async_copy(dq, dq_hbm, sems.at[2]),
-    ]
-    copies[0].start()
-    copies[1].start()
-    dq[...] = (dq_own[...] + dq_far[...].astype(F32)).astype(BF16)
-    copies[2].start()
+def add_queries(own, far, total_hbm, total, sems):
+    copies = []
+    for n in range(2):
+        c = slice(n * WIDTH // 2, (n + 1) * WIDTH // 2)
+        total[:, c] = (own[:, c] + far[:, c].astype(F32)).astype(BF16)
+        copies.append(pltpu.make_async_copy(total.at[:, c], total_hbm.at[:, c], sems.at[n]))
+        copies[n].start()
     for copy in copies:
         copy.wait()
 
@@ -347,14 +342,13 @@
     return lax.ppermute(block, "seq", route)
 
 
-def call(body, name, ins, outs, scratch=(), aliases=None):
+def call(body, name, ins, outs, scratch=()):
     return pl.pallas_call(
         body,
         in_specs=[place for x, place in ins],
         out_specs=[place for shape, kind, place in outs],
         out_shape=[jax.ShapeDtypeStruct(shape, kind) for shape, kind, place in outs],
         scratch_shapes=scratch,
-        input_output_aliases=aliases or {},
         compiler_params=pltpu.CompilerParams(vmem_limit_bytes=20 << 20),
         cost_estimate=pl.CostEstimate(
             flops=1 << 30, bytes_accessed=4 << 20, transcendentals=0
@@ -406,8 +400,7 @@
         [(tokens, BF16, VMEM), (pairs, BF16, VMEM), (pairs, BF16, VMEM)],
     )
     dq_back = passed_along(dq_far, -1)
-    rest = (ROWS, WIDTH - SENT * PAIR)
-    out, dq_own, dk, dv, dk_last, dv_last = call(
+    out, dq_own, dk, dv = call(
         gradients,
         "gradients",
         [
@@ -416,23 +409,19 @@
                 q, g, q_far, g_far, k, w_own, dp_own, p_far, ds_far, numer, message_back, stats
             )
         ],
-        [
-            (tokens, BF16, HBM), (tokens, F32, VMEM), (pool, BF16, HBM), (pool, BF16, HBM),
-            (rest, BF16, VMEM), (rest, BF16, VMEM),
-        ],
+        [(tokens, BF16, HBM), (tokens, F32, VMEM), (pool, BF16, HBM), (pool, BF16, HBM)],
         [
             pltpu.VMEM(tokens, BF16), pltpu.VMEM(pool, BF16), pltpu.VMEM(pool, BF16),
-            dma((1 + 2 * SENT,)),
+            dma((1 + 2 * PAIRS,)),
         ],
     )
-    dk, dv, query_grad = call(
-        last_copies,
-        "last_copies",
-        [(dk, HBM), (dv, HBM)] + [(x, VMEM) for x in (dk_last, dv_last, dq_own, dq_back)],
-        [(pool, BF16, HBM), (pool, BF16, HBM), (tokens, BF16, HBM)],
-        [pltpu.VMEM(tokens, BF16), dma((3,))],
-        {0: 0, 1: 1},
-    )
+    query_grad = call(
+        add_queries,
+        "add_queries",
+        [(dq_own, VMEM), (dq_back, VMEM)],
+        [(tokens, BF16, HBM)],
+        [pltpu.VMEM(tokens, BF16), dma((2,))],
+    )[0]
     return (out, query_grad, dk, dv)
 
 

time: 23.2 us -> 22.9 us (0.987)
  Pallas kernels: 11.8 us -> 11.1 us
  waiting for transfers between devices: 0.13 us -> 0.4 us
    pallas_call x6, Pallas kernels: 11.8 us -> 11.1 us  [call(): pl.pallas_call(body, in_specs=[place for x, place in ins], out_specs=[pla...]
    ppermute x4, waiting for transfers between devices: 0.13 us -> 0.4 us  [passed_along(): return lax.ppermute(block, 'seq', route)]
  transfers between devices with their start and end apart: 4 -> 4, of which waited for: 1 -> 1; matrix products, arithmetic and copies ran while one was open for 0% -> 0% of each run, Pallas kernels for 47% -> 46%
where the time goes in v5:
time: 22.9 us; the launch traced here: 22.8 us
  Pallas kernels  11.1 us (48%)
  starting transfers between devices  10.5 us (46%)
  between operations  0.68 us (3%)
  waiting for transfers between devices  0.4 us (2%)
    pallas_call x6, Pallas kernels, call(): pl.pallas_call(body, in_specs=[place for x, place in ins], out_specs=[pla...  11.1 us
    ppermute x4, starting transfers between devices, passed_along(): return lax.ppermute(block, 'seq', route)  10.5 us
  transfers between devices with their start and end apart: 4, of which 1 were waited for; matrix products, arithmetic and copies ran while one was open for 0% of the time, Pallas kernels for 46%

profile of v5, /device:TPU:1, one launch (start us, length us, event | category | flops | bytes accessed | tf_op | source)
XLA Modules:
  0.0 22.8 jit_solution(8856376457696730071)
XLA Ops:
  0.6 2.7 %collective-permute-start = (bf16[64,2048]{1,0:T(8,128)(2,1)}, bf16[64,2048]{1,0:T(8,128)(2,1)S(1)}, u32[]{:S(2)}, u32[]{:S(2)}) collective-permute-start(bf16[64,2048]{1,0:T(8,128)(2,1)} %q_hbm.1), channel_id=1, source_target_pairs={{31,0},{0,1},{1,2},{2,3},{3,4},{4,5},{5,6},{6,7},{7,8},{8,9},{9,10... | collective-permute-start | bytes 786440 | tf_op jit(solution)/shard_map/ppermute | solution.py:342
  3.3 3.4 %own_forward.1 = (f32[24,128]{1,0:T(8,128)S(1)}, f32[64,2048]{1,0:T(8,128)S(1)}, bf16[512,1024]{1,0:T(8,128)(2,1)S(1)}, bf16[64,2048]{1,0:T(8,128)(2,1)S(1)}, bf...) custom-call(s32[8,32]{1,0:T(8,128)} %bitcast.1, s32[32]{0:T(128)} %counts_hbm.3, ...), custom_call_target="tpu_custom_call" | custom-call | flops 1073741824 | bytes 4194304 | tf_op jit(solution)/shard_map/own_forward/pallas_call | solution.py:346
  6.7 0.1 collective-permute-start.1
  6.8 0.8 %own_dprob.1 = (bf16[512,1024]{1,0:T(8,128)(2,1)S(1)}, f32[8,128]{1,0:T(8,128)S(1)}) custom-call(s32[8,32]{1,0:T(8,128)} %bitcast.2, s32[32]{0:T(128)} %counts_hbm.3, bf16[64,2176]{1,0:T(8,128)(2,1)S(1)} %get-tuple-element.24.g, bf16[512,2048]{1,0:T(8,128)(2,1)S(1)} %get-tuple-element.27.v), custom_call_target="tpu_custom_call" | custom-call | flops 1073741824 | bytes 4194304 | tf_op jit(solution)/shard_map/own_dprob/pallas_call | solution.py:346
  7.7 0.0 collective-permute-done.q.q_far
  7.7 1.4 %far_forward.1 = (bf16[64,2176]{1,0:T(8,128)(2,1)S(1)}, bf16[512,1024]{1,0:T(8,128)(2,1)S(1)}, f32[16,128]{1,0:T(8,128)S(1)}) custom-call(f32[8,128]{1,0:T(8,128)S(1)} %get-tuple-element.29.bias_ref, bf16[64,2048]{1,0:T(8,128)(2,1)S(1)} %collective-permute-done.q.q_far, bf16[512,2048]{1,0:T(8,128)(2,1)S(1)} %get-tuple-element.25.k, ...), custom_call_target="tpu_custom_call" | custom-call | flops 1073741824 | bytes 4194304 | tf_op jit(solution)/shard_map/far_forward/pallas_call | solution.py:346
  9.1 5.7 %collective-permute-start.2 = (bf16[64,2176]{1,0:T(8,128)(2,1)S(1)}, bf16[64,2176]{1,0:T(8,128)(2,1)S(1)}, u32[]{:S(2)}, u32[]{:S(2)}) collective-permute-start(bf16[64,2176]{1,0:T(8,128)(2,1)S(1)} %get-tuple-element.31.message), channel_id=1, source_target_pairs={{1,0},{2,1},{3,2},{4,3},{5,4},{6,5},{7,6},{8,7},{9,8},{10,9},{11,1... | collective-permute-start | bytes 835592 | tf_op jit(solution)/shard_map/ppermute | solution.py:342
  14.8 0.0 collective-permute-done.1.g.g_far
  14.8 1.4 %far_backward.1 = (bf16[64,2048]{1,0:T(8,128)(2,1)S(1)}, bf16[512,1024]{1,0:T(8,128)(2,1)S(1)}, bf16[512,1024]{1,0:T(8,128)(2,1)S(1)}) custom-call(bf16[64,2176]{1,0:T(8,128)(2,1)S(1)} %collective-permute-done.1.g.g_far, bf16[512,2048]{1,0:T(8,128)(2,1)S(1)} %get-tuple-element.25.k, bf16[512,2048]{1,0:T(8,128)(2,1)S(1)} %get-tuple-element.27.v, ...), custom_call_target="tpu_custom_call" | custom-call | flops 1073741824 | bytes 4194304 | tf_op jit(solution)/shard_map/far_backward/pallas_call | solution.py:346
  16.1 2.1 %collective-permute-start.3 = (bf16[64,2048]{1,0:T(8,128)(2,1)S(1)}, bf16[64,2048]{1,0:T(8,128)(2,1)S(1)}, u32[]{:S(2)}, u32[]{:S(2)}) collective-permute-start(bf16[64,2048]{1,0:T(8,128)(2,1)S(1)} %get-tuple-element.39), channel_id=1, source_target_pairs={{1,0},{2,1},{3,2},{4,3},{5,4},{6,5},{7,6},{8,7},{9,8},{10,9},{11,1... | collective-permute-start | bytes 786440 | tf_op jit(solution)/shard_map/ppermute | solution.py:342
  18.2 0.0 collective-permute-done.2.message
  18.2 3.4 %gradients.1 = (bf16[64,2048]{1,0:T(8,128)(2,1)}, f32[64,2048]{1,0:T(8,128)S(1)}, bf16[512,2048]{1,0:T(8,128)(2,1)}, bf16[512,2048]{1,0:T(8,128)(2,1)}) custom-call(bf16[64,2048]{1,0:T(8,128)(2,1)S(1)} %get-tuple-element.23.q, bf16[64,2176]{1,0:T(8,128)(2,1)S(1)} %get-tuple-element.24.g, bf16[64,2048]{1,0:T(8,128)(2,1)S(1)} %collective-permute-done.q.q_far, ...), custom_call_target="tpu_custom_call" | custom-call | flops 1073741824 | bytes 4194304 | tf_op jit(solution)/shard_map/gradients/pallas_call | solution.py:346
  21.6 0.4 %collective-permute-done.3.far = bf16[64,2048]{1,0:T(8,128)(2,1)S(1)} collective-permute-done((bf16[64,2048]{1,0:T(8,128)(2,1)S(1)}, bf16[64,2048]{1,0:T(8,128)(2,1)S(1)}, u32[]{:S(2)}, u32[]{:S(2)}) %collective-permute-start.3) | collective-permute-done | bytes 262176 | tf_op jit(solution)/shard_map/ppermute | solution.py:342
  22.0 0.7 %add_queries.1 = bf16[64,2048]{1,0:T(8,128)(2,1)} custom-call(f32[64,2048]{1,0:T(8,128)S(1)} %get-tuple-element.38.own, bf16[64,2048]{1,0:T(8,128)(2,1)S(1)} %collective-permute-done.3.far), custom_call_target="tpu_custom_call" | custom-call | flops 1073741824 | bytes 4194304 | tf_op jit(solution)/shard_map/add_queries/pallas_call | solution.py:346
Async XLA Ops:
  0.6 7.0 %collective-permute-start = (bf16[64,2048]{1,0:T(8,128)(2,1)}, bf16[64,2048]{1,0:T(8,128)(2,1)S(1)}, u32[]{:S(2)}, u32[]{:S(2)}) collective-permute-start(bf16[64,2048]{1,0:T(8,128)(2,1)} %q_hbm.1), channel_id=1, source_target_pairs={{31,0},{0,1},{1,2},{2,3},{3,4},{4,5},{5,6},{6,7},{7,8},{8,9},{9,10... | collective-permute-start | bytes 786440 | tf_op jit(solution)/shard_map/ppermute | solution.py:342
  6.7 8.0 %collective-permute-start.1 = (bf16[64,2176]{1,0:T(8,128)(2,1)S(1)}, bf16[64,2176]{1,0:T(8,128)(2,1)S(1)}, u32[]{:S(2)}, u32[]{:S(2)}) collective-permute-start(bf16[64,2176]{1,0:T(8,128)(2,1)S(1)} %get-tuple-element.24.g), channel_id=1, source_target_pairs={{31,0},{0,1},{1,2},{2,3},{3,4},{4,5},{5,6},{6,7},{7,8},{8,9},{9,10... | collective-permute-start | bytes 835592 | tf_op jit(solution)/shard_map/ppermute | solution.py:342
  9.1 9.1 %collective-permute-start.2 = (bf16[64,2176]{1,0:T(8,128)(2,1)S(1)}, bf16[64,2176]{1,0:T(8,128)(2,1)S(1)}, u32[]{:S(2)}, u32[]{:S(2)}) collective-permute-start(bf16[64,2176]{1,0:T(8,128)(2,1)S(1)} %get-tuple-element.31.message), channel_id=1, source_target_pairs={{1,0},{2,1},{3,2},{4,3},{5,4},{6,5},{7,6},{8,7},{9,8},{10,9},{11,1... | collective-permute-start | bytes 835592 | tf_op jit(solution)/shard_map/ppermute | solution.py:342
  16.1 5.9 %collective-permute-start.3 = (bf16[64,2048]{1,0:T(8,128)(2,1)S(1)}, bf16[64,2048]{1,0:T(8,128)(2,1)S(1)}, u32[]{:S(2)}, u32[]{:S(2)}) collective-permute-start(bf16[64,2048]{1,0:T(8,128)(2,1)S(1)} %get-tuple-element.39), channel_id=1, source_target_pairs={{1,0},{2,1},{3,2},{4,3},{5,4},{6,5},{7,6},{8,7},{9,8},{10,9},{11,1... | collective-permute-start | bytes 786440 | tf_op jit(solution)/shard_map/ppermute | solution.py:342

commit v6 on v5

--- a/solution.py
+++ b/solution.py
@@ -99,10 +99,10 @@
     return ([x.astype(BF16) for x in e], peak, (sums[0] + sums[1]) + (sums[2] + sums[3]))
 
 
-def staggered(stages):
+def staggered(stages, lags):
     held = {}
-    for t in range(PAIRS + len(stages) - 1):
-        for lag, stage in enumerate(stages):
+    for t in range(PAIRS + lags[-1]):
+        for stage, lag in zip(stages, lags):
             p = t - lag
             if 0 <= p < PAIRS:
                 held[p] = stage(p, held.get(p))
@@ -196,7 +196,7 @@
     def dots(p, part):
         stats[16 + p : 17 + p, :] = head_sums_by_transpose(part * g[:, wide(p)].astype(F32))
 
-    staggered([scores, softmax, sums, dots])
+    staggered([scores, softmax, sums, dots], (0, 1, 2, 3))
     g[:, WIDTH:] = packed([(stats[:8, :], 3), (stats[8:16, :], 2), (stats[16:, :], 2)])
 
 
@@ -241,7 +241,7 @@
         part = dot(jnp.concatenate(e, 0), v[:, wide(p)], TN)
         message[:, wide(p)] = own_columns(part).astype(BF16)
 
-    staggered([scores, softmax, sums])
+    staggered([scores, softmax, sums], (0, 3, 7))
     message[:, WIDTH:] = packed([(stats[:8, :], 3), (stats[8:, :], 2)])
 
 
@@ -271,7 +271,7 @@
         part = own_columns(dot(jnp.concatenate(ds, 0), k[:, wide(p)], TN))
         dq[:, wide(p)] = (part * SCALE).astype(BF16)
 
-    staggered([dprobs, dscores, dqueries])
+    staggered([dprobs, dscores, dqueries], (0, 2, 5))
 
 
 def gradients(
@@ -283,6 +283,7 @@
     own, far = merged(stats[0:8, :], stats[8:16, :], peak_far, total_far)
     factors = as_columns([own, far])
     copies = []
+    own_ds = []
 
     def send(x, to):
         copies.append(pltpu.make_async_copy(x, to, sems.at[len(copies)]))
@@ -308,7 +309,7 @@
     def sums(p, held):
         pr, ds = held
         c, h = wide(p), half(p)
-        dq[:, c] = own_columns(dot(ds, k[:, c], TN)) * SCALE
+        own_ds.append(ds)
         p_all = jnp.concatenate([pr, p_far[:, h]], 1)
         ds_all = jnp.concatenate([ds, ds_far[:, h]], 1)
         g_all = jnp.concatenate([two_heads(g[:, c]), two_heads(g_far[:, c])], 0)
@@ -320,7 +321,9 @@
         send(dv.at[:, c], dv_hbm.at[:, c])
         send(dk.at[:, c], dk_hbm.at[:, c])
 
-    staggered([merge, dscores, sums])
+    staggered([merge, dscores, sums], (0, 1, 2))
+    for p, ds in enumerate(own_ds):
+        dq[:, wide(p)] = own_columns(dot(ds, k[:, wide(p)], TN)) * SCALE
     for copy in copies:
         copy.wait()
 

time: 22.9 us -> 22.6 us (0.987)
  Pallas kernels: 11.1 us -> 10.7 us
  starting transfers between devices: 10.5 us -> 10.8 us
    pallas_call x6, Pallas kernels: 11.1 us -> 10.7 us  [call(): pl.pallas_call(body, in_specs=[place for x, place in ins], out_specs=[pla...]
    ppermute x4, starting transfers between devices: 10.5 us -> 10.8 us  [passed_along(): return lax.ppermute(block, 'seq', route)]
  transfers between devices with their start and end apart: 4 -> 4, of which waited for: 1 -> 1; matrix products, arithmetic and copies ran while one was open for 0% -> 0% of each run, Pallas kernels for 46% -> 44%
where the time goes in v6:
time: 22.6 us; the launch traced here: 22.5 us
  starting transfers between devices  10.8 us (48%)
  Pallas kernels  10.7 us (47%)
  between operations  0.68 us (3%)
  waiting for transfers between devices  0.36 us (2%)
    ppermute x4, starting transfers between devices, passed_along(): return lax.ppermute(block, 'seq', route)  10.8 us
    pallas_call x6, Pallas kernels, call(): pl.pallas_call(body, in_specs=[place for x, place in ins], out_specs=[pla...  10.7 us
  transfers between devices with their start and end apart: 4, of which 1 were waited for; matrix products, arithmetic and copies ran while one was open for 0% of the time, Pallas kernels for 44%

profile of v6, /device:TPU:1, one launch (start us, length us, event | category | flops | bytes accessed | tf_op | source)
XLA Modules:
  0.0 22.5 jit_solution(2218860350795163908)
XLA Ops:
  0.6 2.7 %collective-permute-start = (bf16[64,2048]{1,0:T(8,128)(2,1)}, bf16[64,2048]{1,0:T(8,128)(2,1)S(1)}, u32[]{:S(2)}, u32[]{:S(2)}) collective-permute-start(bf16[64,2048]{1,0:T(8,128)(2,1)} %q_hbm.1), channel_id=1, source_target_pairs={{31,0},{0,1},{1,2},{2,3},{3,4},{4,5},{5,6},{6,7},{7,8},{8,9},{9,10... | collective-permute-start | bytes 786440 | tf_op jit(solution)/shard_map/ppermute | solution.py:345
  3.3 3.4 %own_forward.1 = (f32[24,128]{1,0:T(8,128)S(1)}, f32[64,2048]{1,0:T(8,128)S(1)}, bf16[512,1024]{1,0:T(8,128)(2,1)S(1)}, bf16[64,2048]{1,0:T(8,128)(2,1)S(1)}, bf...) custom-call(s32[8,32]{1,0:T(8,128)} %bitcast.1, s32[32]{0:T(128)} %counts_hbm.3, ...), custom_call_target="tpu_custom_call" | custom-call | flops 1073741824 | bytes 4194304 | tf_op jit(solution)/shard_map/own_forward/pallas_call | solution.py:349
  6.7 0.1 collective-permute-start.1
  6.8 0.8 %own_dprob.1 = (bf16[512,1024]{1,0:T(8,128)(2,1)S(1)}, f32[8,128]{1,0:T(8,128)S(1)}) custom-call(s32[8,32]{1,0:T(8,128)} %bitcast.2, s32[32]{0:T(128)} %counts_hbm.3, bf16[64,2176]{1,0:T(8,128)(2,1)S(1)} %get-tuple-element.24.g, bf16[512,2048]{1,0:T(8,128)(2,1)S(1)} %get-tuple-element.27.v), custom_call_target="tpu_custom_call" | custom-call | flops 1073741824 | bytes 4194304 | tf_op jit(solution)/shard_map/own_dprob/pallas_call | solution.py:349
  7.7 0.0 collective-permute-done.q.q_far
  7.7 1.2 %far_forward.1 = (bf16[64,2176]{1,0:T(8,128)(2,1)S(1)}, bf16[512,1024]{1,0:T(8,128)(2,1)S(1)}, f32[16,128]{1,0:T(8,128)S(1)}) custom-call(f32[8,128]{1,0:T(8,128)S(1)} %get-tuple-element.29.bias_ref, bf16[64,2048]{1,0:T(8,128)(2,1)S(1)} %collective-permute-done.q.q_far, bf16[512,2048]{1,0:T(8,128)(2,1)S(1)} %get-tuple-element.25.k, ...), custom_call_target="tpu_custom_call" | custom-call | flops 1073741824 | bytes 4194304 | tf_op jit(solution)/shard_map/far_forward/pallas_call | solution.py:349
  8.9 5.7 %collective-permute-start.2 = (bf16[64,2176]{1,0:T(8,128)(2,1)S(1)}, bf16[64,2176]{1,0:T(8,128)(2,1)S(1)}, u32[]{:S(2)}, u32[]{:S(2)}) collective-permute-start(bf16[64,2176]{1,0:T(8,128)(2,1)S(1)} %get-tuple-element.31.message), channel_id=1, source_target_pairs={{1,0},{2,1},{3,2},{4,3},{5,4},{6,5},{7,6},{8,7},{9,8},{10,9},{11,1... | collective-permute-start | bytes 835592 | tf_op jit(solution)/shard_map/ppermute | solution.py:345
  14.5 0.0 collective-permute-done.1.g.g_far
  14.5 1.3 %far_backward.1 = (bf16[64,2048]{1,0:T(8,128)(2,1)S(1)}, bf16[512,1024]{1,0:T(8,128)(2,1)S(1)}, bf16[512,1024]{1,0:T(8,128)(2,1)S(1)}) custom-call(bf16[64,2176]{1,0:T(8,128)(2,1)S(1)} %collective-permute-done.1.g.g_far, bf16[512,2048]{1,0:T(8,128)(2,1)S(1)} %get-tuple-element.25.k, bf16[512,2048]{1,0:T(8,128)(2,1)S(1)} %get-tuple-element.27.v, ...), custom_call_target="tpu_custom_call" | custom-call | flops 1073741824 | bytes 4194304 | tf_op jit(solution)/shard_map/far_backward/pallas_call | solution.py:349
  15.9 2.3 %collective-permute-start.3 = (bf16[64,2048]{1,0:T(8,128)(2,1)S(1)}, bf16[64,2048]{1,0:T(8,128)(2,1)S(1)}, u32[]{:S(2)}, u32[]{:S(2)}) collective-permute-start(bf16[64,2048]{1,0:T(8,128)(2,1)S(1)} %get-tuple-element.39), channel_id=1, source_target_pairs={{1,0},{2,1},{3,2},{4,3},{5,4},{6,5},{7,6},{8,7},{9,8},{10,9},{11,1... | collective-permute-start | bytes 786440 | tf_op jit(solution)/shard_map/ppermute | solution.py:345
  18.2 0.0 collective-permute-done.2.message
  18.2 3.2 %gradients.1 = (bf16[64,2048]{1,0:T(8,128)(2,1)}, f32[64,2048]{1,0:T(8,128)S(1)}, bf16[512,2048]{1,0:T(8,128)(2,1)}, bf16[512,2048]{1,0:T(8,128)(2,1)}) custom-call(bf16[64,2048]{1,0:T(8,128)(2,1)S(1)} %get-tuple-element.23.q, bf16[64,2176]{1,0:T(8,128)(2,1)S(1)} %get-tuple-element.24.g, bf16[64,2048]{1,0:T(8,128)(2,1)S(1)} %collective-permute-done.q.q_far, ...), custom_call_target="tpu_custom_call" | custom-call | flops 1073741824 | bytes 4194304 | tf_op jit(solution)/shard_map/gradients/pallas_call | solution.py:349
  21.4 0.4 %collective-permute-done.3.far = bf16[64,2048]{1,0:T(8,128)(2,1)S(1)} collective-permute-done((bf16[64,2048]{1,0:T(8,128)(2,1)S(1)}, bf16[64,2048]{1,0:T(8,128)(2,1)S(1)}, u32[]{:S(2)}, u32[]{:S(2)}) %collective-permute-start.3) | collective-permute-done | bytes 262176 | tf_op jit(solution)/shard_map/ppermute | solution.py:345
  21.7 0.7 %add_queries.1 = bf16[64,2048]{1,0:T(8,128)(2,1)} custom-call(f32[64,2048]{1,0:T(8,128)S(1)} %get-tuple-element.38.own, bf16[64,2048]{1,0:T(8,128)(2,1)S(1)} %collective-permute-done.3.far), custom_call_target="tpu_custom_call" | custom-call | flops 1073741824 | bytes 4194304 | tf_op jit(solution)/shard_map/add_queries/pallas_call | solution.py:349
Async XLA Ops:
  0.6 7.0 %collective-permute-start = (bf16[64,2048]{1,0:T(8,128)(2,1)}, bf16[64,2048]{1,0:T(8,128)(2,1)S(1)}, u32[]{:S(2)}, u32[]{:S(2)}) collective-permute-start(bf16[64,2048]{1,0:T(8,128)(2,1)} %q_hbm.1), channel_id=1, source_target_pairs={{31,0},{0,1},{1,2},{2,3},{3,4},{4,5},{5,6},{6,7},{7,8},{8,9},{9,10... | collective-permute-start | bytes 786440 | tf_op jit(solution)/shard_map/ppermute | solution.py:345
  6.7 7.8 %collective-permute-start.1 = (bf16[64,2176]{1,0:T(8,128)(2,1)S(1)}, bf16[64,2176]{1,0:T(8,128)(2,1)S(1)}, u32[]{:S(2)}, u32[]{:S(2)}) collective-permute-start(bf16[64,2176]{1,0:T(8,128)(2,1)S(1)} %get-tuple-element.24.g), channel_id=1, source_target_pairs={{31,0},{0,1},{1,2},{2,3},{3,4},{4,5},{5,6},{6,7},{7,8},{8,9},{9,10... | collective-permute-start | bytes 835592 | tf_op jit(solution)/shard_map/ppermute | solution.py:345
  8.9 9.3 %collective-permute-start.2 = (bf16[64,2176]{1,0:T(8,128)(2,1)S(1)}, bf16[64,2176]{1,0:T(8,128)(2,1)S(1)}, u32[]{:S(2)}, u32[]{:S(2)}) collective-permute-start(bf16[64,2176]{1,0:T(8,128)(2,1)S(1)} %get-tuple-element.31.message), channel_id=1, source_target_pairs={{1,0},{2,1},{3,2},{4,3},{5,4},{6,5},{7,6},{8,7},{9,8},{10,9},{11,1... | collective-permute-start | bytes 835592 | tf_op jit(solution)/shard_map/ppermute | solution.py:345
  15.9 5.9 %collective-permute-start.3 = (bf16[64,2048]{1,0:T(8,128)(2,1)S(1)}, bf16[64,2048]{1,0:T(8,128)(2,1)S(1)}, u32[]{:S(2)}, u32[]{:S(2)}) collective-permute-start(bf16[64,2048]{1,0:T(8,128)(2,1)S(1)} %get-tuple-element.39), channel_id=1, source_target_pairs={{1,0},{2,1},{3,2},{4,3},{5,4},{6,5},{7,6},{8,7},{9,8},{10,9},{11,1... | collective-permute-start | bytes 786440 | tf_op jit(solution)/shard_map/ppermute | solution.py:345

commit v7 on v6

--- a/solution.py
+++ b/solution.py
@@ -245,10 +245,11 @@
     message[:, WIDTH:] = packed([(stats[:8, :], 3), (stats[8:, :], 2)])
 
 
-def far_backward(g, k, v, weights, message, stats, dq, prob, dscore):
+def far_backward(g, k, v, weights, message, stats, dq, dscore, factor):
     peak_own, total_own, dot_own = unpacked(g[:, WIDTH:], (3, 2, 2))
     own, far = merged(peak_own, total_own, stats[0:8, :], stats[8:16, :])
     delta_own = own * dot_own
+    factor[...] = far
 
     def dprobs(p, _):
         gg = g[:, wide(p)]
@@ -263,7 +264,6 @@
             r, h = rows_of(n), half(p)
             pr = weights[r, h].astype(F32) * far[p : p + 1]
             out.append((pr * (dp[n] - delta)).astype(BF16))
-            prob[r, h] = pr.astype(BF16)
             dscore[r, h] = out[n]
         return out
 
@@ -275,7 +275,7 @@
 
 
 def gradients(
-    q, g, q_far, g_far, k, w_own, dp_own, p_far, ds_far, numer, message, stats,
+    q, g, q_far, g_far, k, w_own, dp_own, w_far, ds_far, f_far, numer, message, stats,
     out_hbm, dq, dk_hbm, dv_hbm,
     out, dk, dv, sems,
 ):
@@ -310,7 +310,8 @@
         pr, ds = held
         c, h = wide(p), half(p)
         own_ds.append(ds)
-        p_all = jnp.concatenate([pr, p_far[:, h]], 1)
+        pr_far = (w_far[:, h].astype(F32) * f_far[p : p + 1, :]).astype(BF16)
+        p_all = jnp.concatenate([pr, pr_far], 1)
         ds_all = jnp.concatenate([ds, ds_far[:, h]], 1)
         g_all = jnp.concatenate([two_heads(g[:, c]), two_heads(g_far[:, c])], 0)
         q_all = jnp.concatenate([two_heads(q[:, c]), two_heads(q_far[:, c])], 0)
@@ -396,11 +397,11 @@
         [(longer, BF16, VMEM), (pairs, BF16, VMEM), ((16, HD), F32, VMEM)],
     )
     message_back = passed_along(message, -1)
-    dq_far, p_far, ds_far = call(
+    dq_far, ds_far, f_far = call(
         far_backward,
         "far_backward",
         [(x, VMEM) for x in (g_far, k, v, w_far, message, stats_far)],
-        [(tokens, BF16, VMEM), (pairs, BF16, VMEM), (pairs, BF16, VMEM)],
+        [(tokens, BF16, VMEM), (pairs, BF16, VMEM), ((8, HD), F32, VMEM)],
     )
     dq_back = passed_along(dq_far, -1)
     out, dq_own, dk, dv = call(
@@ -409,7 +410,7 @@
         [
             (x, VMEM)
             for x in (
-                q, g, q_far, g_far, k, w_own, dp_own, p_far, ds_far, numer, message_back, stats
+                q, g, q_far, g_far, k, w_own, dp_own, w_far, ds_far, f_far, numer, message_back, stats
             )
         ],
         [(tokens, BF16, HBM), (tokens, F32, VMEM), (pool, BF16, HBM), (pool, BF16, HBM)],

time: 22.6 us -> 22.5 us (level)
  no operation moved by 1% of the time
where the time goes in v7:
time: 22.5 us; the launch traced here: 22.3 us
  starting transfers between devices  10.8 us (48%)
  Pallas kernels  10.5 us (47%)
  between operations  0.68 us (3%)
  waiting for transfers between devices  0.35 us (2%)
    ppermute x4, starting transfers between devices, passed_along(): return lax.ppermute(block, 'seq', route)  10.8 us
    pallas_call x6, Pallas kernels, call(): pl.pallas_call(body, in_specs=[place for x, place in ins], out_specs=[pla...  10.5 us
  transfers between devices with their start and end apart: 4, of which 1 were waited for; matrix products, arithmetic and copies ran while one was open for 0% of the time, Pallas kernels for 44%

profile of v7, /device:TPU:1, one launch (start us, length us, event | category | flops | bytes accessed | tf_op | source)
XLA Modules:
  0.0 22.3 jit_solution(12595093653354720540)
XLA Ops:
  0.6 2.7 %collective-permute-start = (bf16[64,2048]{1,0:T(8,128)(2,1)}, bf16[64,2048]{1,0:T(8,128)(2,1)S(1)}, u32[]{:S(2)}, u32[]{:S(2)}) collective-permute-start(bf16[64,2048]{1,0:T(8,128)(2,1)} %q_hbm.1), channel_id=1, source_target_pairs={{31,0},{0,1},{1,2},{2,3},{3,4},{4,5},{5,6},{6,7},{7,8},{8,9},{9,10... | collective-permute-start | bytes 786440 | tf_op jit(solution)/shard_map/ppermute | solution.py:346
  3.3 3.4 %own_forward.1 = (f32[24,128]{1,0:T(8,128)S(1)}, f32[64,2048]{1,0:T(8,128)S(1)}, bf16[512,1024]{1,0:T(8,128)(2,1)S(1)}, bf16[64,2048]{1,0:T(8,128)(2,1)S(1)}, bf...) custom-call(s32[8,32]{1,0:T(8,128)} %bitcast.1, s32[32]{0:T(128)} %counts_hbm.3, ...), custom_call_target="tpu_custom_call" | custom-call | flops 1073741824 | bytes 4194304 | tf_op jit(solution)/shard_map/own_forward/pallas_call | solution.py:350
  6.7 0.1 collective-permute-start.1
  6.8 0.8 %own_dprob.1 = (bf16[512,1024]{1,0:T(8,128)(2,1)S(1)}, f32[8,128]{1,0:T(8,128)S(1)}) custom-call(s32[8,32]{1,0:T(8,128)} %bitcast.2, s32[32]{0:T(128)} %counts_hbm.3, bf16[64,2176]{1,0:T(8,128)(2,1)S(1)} %get-tuple-element.24.g, bf16[512,2048]{1,0:T(8,128)(2,1)S(1)} %get-tuple-element.27.v), custom_call_target="tpu_custom_call" | custom-call | flops 1073741824 | bytes 4194304 | tf_op jit(solution)/shard_map/own_dprob/pallas_call | solution.py:350
  7.7 0.0 collective-permute-done.q.q_far
  7.7 1.1 %far_forward.1 = (bf16[64,2176]{1,0:T(8,128)(2,1)S(1)}, bf16[512,1024]{1,0:T(8,128)(2,1)S(1)}, f32[16,128]{1,0:T(8,128)S(1)}) custom-call(f32[8,128]{1,0:T(8,128)S(1)} %get-tuple-element.29.bias_ref, bf16[64,2048]{1,0:T(8,128)(2,1)S(1)} %collective-permute-done.q.q_far, bf16[512,2048]{1,0:T(8,128)(2,1)S(1)} %get-tuple-element.25.k, ...), custom_call_target="tpu_custom_call" | custom-call | flops 1073741824 | bytes 4194304 | tf_op jit(solution)/shard_map/far_forward/pallas_call | solution.py:350
  8.8 5.7 %collective-permute-start.2 = (bf16[64,2176]{1,0:T(8,128)(2,1)S(1)}, bf16[64,2176]{1,0:T(8,128)(2,1)S(1)}, u32[]{:S(2)}, u32[]{:S(2)}) collective-permute-start(bf16[64,2176]{1,0:T(8,128)(2,1)S(1)} %get-tuple-element.31.message), channel_id=1, source_target_pairs={{1,0},{2,1},{3,2},{4,3},{5,4},{6,5},{7,6},{8,7},{9,8},{10,9},{11,1... | collective-permute-start | bytes 835592 | tf_op jit(solution)/shard_map/ppermute | solution.py:346
  14.5 0.0 collective-permute-done.1.g.g_far
  14.5 1.2 %far_backward.1 = (bf16[64,2048]{1,0:T(8,128)(2,1)S(1)}, bf16[512,1024]{1,0:T(8,128)(2,1)S(1)}, f32[8,128]{1,0:T(8,128)S(1)}) custom-call(bf16[64,2176]{1,0:T(8,128)(2,1)S(1)} %collective-permute-done.1.g.g_far, bf16[512,2048]{1,0:T(8,128)(2,1)S(1)} %get-tuple-element.25.k, bf16[512,2048]{1,0:T(8,128)(2,1)S(1)} %get-tuple-element.27.v, ...), custom_call_target="tpu_custom_call" | custom-call | flops 1073741824 | bytes 4194304 | tf_op jit(solution)/shard_map/far_backward/pallas_call | solution.py:350
  15.7 2.4 %collective-permute-start.3 = (bf16[64,2048]{1,0:T(8,128)(2,1)S(1)}, bf16[64,2048]{1,0:T(8,128)(2,1)S(1)}, u32[]{:S(2)}, u32[]{:S(2)}) collective-permute-start(bf16[64,2048]{1,0:T(8,128)(2,1)S(1)} %get-tuple-element.39), channel_id=1, source_target_pairs={{1,0},{2,1},{3,2},{4,3},{5,4},{6,5},{7,6},{8,7},{9,8},{10,9},{11,1... | collective-permute-start | bytes 786440 | tf_op jit(solution)/shard_map/ppermute | solution.py:346
  18.1 0.0 collective-permute-done.2.message
  18.1 3.2 %gradients.1 = (bf16[64,2048]{1,0:T(8,128)(2,1)}, f32[64,2048]{1,0:T(8,128)S(1)}, bf16[512,2048]{1,0:T(8,128)(2,1)}, bf16[512,2048]{1,0:T(8,128)(2,1)}) custom-call(bf16[64,2048]{1,0:T(8,128)(2,1)S(1)} %get-tuple-element.23.q, bf16[64,2176]{1,0:T(8,128)(2,1)S(1)} %get-tuple-element.24.g, bf16[64,2048]{1,0:T(8,128)(2,1)S(1)} %collective-permute-done.q.q_far, ...), custom_call_target="tpu_custom_call" | custom-call | flops 1073741824 | bytes 4194304 | tf_op jit(solution)/shard_map/gradients/pallas_call | solution.py:350
  21.2 0.3 %collective-permute-done.3.far = bf16[64,2048]{1,0:T(8,128)(2,1)S(1)} collective-permute-done((bf16[64,2048]{1,0:T(8,128)(2,1)S(1)}, bf16[64,2048]{1,0:T(8,128)(2,1)S(1)}, u32[]{:S(2)}, u32[]{:S(2)}) %collective-permute-start.3) | collective-permute-done | bytes 262176 | tf_op jit(solution)/shard_map/ppermute | solution.py:346
  21.6 0.7 %add_queries.1 = bf16[64,2048]{1,0:T(8,128)(2,1)} custom-call(f32[64,2048]{1,0:T(8,128)S(1)} %get-tuple-element.38.own, bf16[64,2048]{1,0:T(8,128)(2,1)S(1)} %collective-permute-done.3.far), custom_call_target="tpu_custom_call" | custom-call | flops 1073741824 | bytes 4194304 | tf_op jit(solution)/shard_map/add_queries/pallas_call | solution.py:350
Async XLA Ops:
  0.6 7.0 %collective-permute-start = (bf16[64,2048]{1,0:T(8,128)(2,1)}, bf16[64,2048]{1,0:T(8,128)(2,1)S(1)}, u32[]{:S(2)}, u32[]{:S(2)}) collective-permute-start(bf16[64,2048]{1,0:T(8,128)(2,1)} %q_hbm.1), channel_id=1, source_target_pairs={{31,0},{0,1},{1,2},{2,3},{3,4},{4,5},{5,6},{6,7},{7,8},{8,9},{9,10... | collective-permute-start | bytes 786440 | tf_op jit(solution)/shard_map/ppermute | solution.py:346
  6.7 7.8 %collective-permute-start.1 = (bf16[64,2176]{1,0:T(8,128)(2,1)S(1)}, bf16[64,2176]{1,0:T(8,128)(2,1)S(1)}, u32[]{:S(2)}, u32[]{:S(2)}) collective-permute-start(bf16[64,2176]{1,0:T(8,128)(2,1)S(1)} %get-tuple-element.24.g), channel_id=1, source_target_pairs={{31,0},{0,1},{1,2},{2,3},{3,4},{4,5},{5,6},{6,7},{7,8},{8,9},{9,10... | collective-permute-start | bytes 835592 | tf_op jit(solution)/shard_map/ppermute | solution.py:346
  8.8 9.3 %collective-permute-start.2 = (bf16[64,2176]{1,0:T(8,128)(2,1)S(1)}, bf16[64,2176]{1,0:T(8,128)(2,1)S(1)}, u32[]{:S(2)}, u32[]{:S(2)}) collective-permute-start(bf16[64,2176]{1,0:T(8,128)(2,1)S(1)} %get-tuple-element.31.message), channel_id=1, source_target_pairs={{1,0},{2,1},{3,2},{4,3},{5,4},{6,5},{7,6},{8,7},{9,8},{10,9},{11,1... | collective-permute-start | bytes 835592 | tf_op jit(solution)/shard_map/ppermute | solution.py:346
  15.7 5.9 %collective-permute-start.3 = (bf16[64,2048]{1,0:T(8,128)(2,1)S(1)}, bf16[64,2048]{1,0:T(8,128)(2,1)S(1)}, u32[]{:S(2)}, u32[]{:S(2)}) collective-permute-start(bf16[64,2048]{1,0:T(8,128)(2,1)S(1)} %get-tuple-element.39), channel_id=1, source_target_pairs={{1,0},{2,1},{3,2},{4,3},{5,4},{6,5},{7,6},{8,7},{9,8},{10,9},{11,1... | collective-permute-start | bytes 786440 | tf_op jit(solution)/shard_map/ppermute | solution.py:346

commit v8 on v7

--- a/solution.py
+++ b/solution.py
@@ -271,7 +271,7 @@
         part = own_columns(dot(jnp.concatenate(ds, 0), k[:, wide(p)], TN))
         dq[:, wide(p)] = (part * SCALE).astype(BF16)
 
-    staggered([dprobs, dscores, dqueries], (0, 2, 5))
+    staggered([dprobs, dscores, dqueries], (0, 3, 6))
 
 
 def gradients(

time: 22.5 us -> 22.5 us (level)
  no operation moved by 1% of the time
where the time goes in v8:
time: 22.5 us; the launch traced here: 22.3 us
  starting transfers between devices  10.8 us (48%)
  Pallas kernels  10.5 us (47%)
  between operations  0.68 us (3%)
  waiting for transfers between devices  0.35 us (2%)
    ppermute x4, starting transfers between devices, passed_along(): return lax.ppermute(block, 'seq', route)  10.8 us
    pallas_call x6, Pallas kernels, call(): pl.pallas_call(body, in_specs=[place for x, place in ins], out_specs=[pla...  10.5 us
  transfers between devices with their start and end apart: 4, of which 1 were waited for; matrix products, arithmetic and copies ran while one was open for 0% of the time, Pallas kernels for 44%

profile of v8, /device:TPU:1, one launch (start us, length us, event | category | flops | bytes accessed | tf_op | source)
XLA Modules:
  0.0 22.3 jit_solution(2079288450024710927)
XLA Ops:
  0.6 2.7 %collective-permute-start = (bf16[64,2048]{1,0:T(8,128)(2,1)}, bf16[64,2048]{1,0:T(8,128)(2,1)S(1)}, u32[]{:S(2)}, u32[]{:S(2)}) collective-permute-start(bf16[64,2048]{1,0:T(8,128)(2,1)} %q_hbm.1), channel_id=1, source_target_pairs={{31,0},{0,1},{1,2},{2,3},{3,4},{4,5},{5,6},{6,7},{7,8},{8,9},{9,10... | collective-permute-start | bytes 786440 | tf_op jit(solution)/shard_map/ppermute | solution.py:346
  3.3 3.4 %own_forward.1 = (f32[24,128]{1,0:T(8,128)S(1)}, f32[64,2048]{1,0:T(8,128)S(1)}, bf16[512,1024]{1,0:T(8,128)(2,1)S(1)}, bf16[64,2048]{1,0:T(8,128)(2,1)S(1)}, bf...) custom-call(s32[8,32]{1,0:T(8,128)} %bitcast.1, s32[32]{0:T(128)} %counts_hbm.3, ...), custom_call_target="tpu_custom_call" | custom-call | flops 1073741824 | bytes 4194304 | tf_op jit(solution)/shard_map/own_forward/pallas_call | solution.py:350
  6.7 0.1 collective-permute-start.1
  6.8 0.8 %own_dprob.1 = (bf16[512,1024]{1,0:T(8,128)(2,1)S(1)}, f32[8,128]{1,0:T(8,128)S(1)}) custom-call(s32[8,32]{1,0:T(8,128)} %bitcast.2, s32[32]{0:T(128)} %counts_hbm.3, bf16[64,2176]{1,0:T(8,128)(2,1)S(1)} %get-tuple-element.24.g, bf16[512,2048]{1,0:T(8,128)(2,1)S(1)} %get-tuple-element.27.v), custom_call_target="tpu_custom_call" | custom-call | flops 1073741824 | bytes 4194304 | tf_op jit(solution)/shard_map/own_dprob/pallas_call | solution.py:350
  7.7 0.0 collective-permute-done.q.q_far
  7.7 1.1 %far_forward.1 = (bf16[64,2176]{1,0:T(8,128)(2,1)S(1)}, bf16[512,1024]{1,0:T(8,128)(2,1)S(1)}, f32[16,128]{1,0:T(8,128)S(1)}) custom-call(f32[8,128]{1,0:T(8,128)S(1)} %get-tuple-element.29.bias_ref, bf16[64,2048]{1,0:T(8,128)(2,1)S(1)} %collective-permute-done.q.q_far, bf16[512,2048]{1,0:T(8,128)(2,1)S(1)} %get-tuple-element.25.k, ...), custom_call_target="tpu_custom_call" | custom-call | flops 1073741824 | bytes 4194304 | tf_op jit(solution)/shard_map/far_forward/pallas_call | solution.py:350
  8.8 5.7 %collective-permute-start.2 = (bf16[64,2176]{1,0:T(8,128)(2,1)S(1)}, bf16[64,2176]{1,0:T(8,128)(2,1)S(1)}, u32[]{:S(2)}, u32[]{:S(2)}) collective-permute-start(bf16[64,2176]{1,0:T(8,128)(2,1)S(1)} %get-tuple-element.31.message), channel_id=1, source_target_pairs={{1,0},{2,1},{3,2},{4,3},{5,4},{6,5},{7,6},{8,7},{9,8},{10,9},{11,1... | collective-permute-start | bytes 835592 | tf_op jit(solution)/shard_map/ppermute | solution.py:346
  14.5 0.0 collective-permute-done.1.g.g_far
  14.5 1.2 %far_backward.1 = (bf16[64,2048]{1,0:T(8,128)(2,1)S(1)}, bf16[512,1024]{1,0:T(8,128)(2,1)S(1)}, f32[8,128]{1,0:T(8,128)S(1)}) custom-call(bf16[64,2176]{1,0:T(8,128)(2,1)S(1)} %collective-permute-done.1.g.g_far, bf16[512,2048]{1,0:T(8,128)(2,1)S(1)} %get-tuple-element.25.k, bf16[512,2048]{1,0:T(8,128)(2,1)S(1)} %get-tuple-element.27.v, ...), custom_call_target="tpu_custom_call" | custom-call | flops 1073741824 | bytes 4194304 | tf_op jit(solution)/shard_map/far_backward/pallas_call | solution.py:350
  15.7 2.4 %collective-permute-start.3 = (bf16[64,2048]{1,0:T(8,128)(2,1)S(1)}, bf16[64,2048]{1,0:T(8,128)(2,1)S(1)}, u32[]{:S(2)}, u32[]{:S(2)}) collective-permute-start(bf16[64,2048]{1,0:T(8,128)(2,1)S(1)} %get-tuple-element.39), channel_id=1, source_target_pairs={{1,0},{2,1},{3,2},{4,3},{5,4},{6,5},{7,6},{8,7},{9,8},{10,9},{11,1... | collective-permute-start | bytes 786440 | tf_op jit(solution)/shard_map/ppermute | solution.py:346
  18.1 0.0 collective-permute-done.2.message
  18.1 3.2 %gradients.1 = (bf16[64,2048]{1,0:T(8,128)(2,1)}, f32[64,2048]{1,0:T(8,128)S(1)}, bf16[512,2048]{1,0:T(8,128)(2,1)}, bf16[512,2048]{1,0:T(8,128)(2,1)}) custom-call(bf16[64,2048]{1,0:T(8,128)(2,1)S(1)} %get-tuple-element.23.q, bf16[64,2176]{1,0:T(8,128)(2,1)S(1)} %get-tuple-element.24.g, bf16[64,2048]{1,0:T(8,128)(2,1)S(1)} %collective-permute-done.q.q_far, ...), custom_call_target="tpu_custom_call" | custom-call | flops 1073741824 | bytes 4194304 | tf_op jit(solution)/shard_map/gradients/pallas_call | solution.py:350
  21.2 0.3 %collective-permute-done.3.far = bf16[64,2048]{1,0:T(8,128)(2,1)S(1)} collective-permute-done((bf16[64,2048]{1,0:T(8,128)(2,1)S(1)}, bf16[64,2048]{1,0:T(8,128)(2,1)S(1)}, u32[]{:S(2)}, u32[]{:S(2)}) %collective-permute-start.3) | collective-permute-done | bytes 262176 | tf_op jit(solution)/shard_map/ppermute | solution.py:346
  21.6 0.7 %add_queries.1 = bf16[64,2048]{1,0:T(8,128)(2,1)} custom-call(f32[64,2048]{1,0:T(8,128)S(1)} %get-tuple-element.38.own, bf16[64,2048]{1,0:T(8,128)(2,1)S(1)} %collective-permute-done.3.far), custom_call_target="tpu_custom_call" | custom-call | flops 1073741824 | bytes 4194304 | tf_op jit(solution)/shard_map/add_queries/pallas_call | solution.py:350
Async XLA Ops:
  0.6 7.0 %collective-permute-start = (bf16[64,2048]{1,0:T(8,128)(2,1)}, bf16[64,2048]{1,0:T(8,128)(2,1)S(1)}, u32[]{:S(2)}, u32[]{:S(2)}) collective-permute-start(bf16[64,2048]{1,0:T(8,128)(2,1)} %q_hbm.1), channel_id=1, source_target_pairs={{31,0},{0,1},{1,2},{2,3},{3,4},{4,5},{5,6},{6,7},{7,8},{8,9},{9,10... | collective-permute-start | bytes 786440 | tf_op jit(solution)/shard_map/ppermute | solution.py:346
  6.7 7.8 %collective-permute-start.1 = (bf16[64,2176]{1,0:T(8,128)(2,1)S(1)}, bf16[64,2176]{1,0:T(8,128)(2,1)S(1)}, u32[]{:S(2)}, u32[]{:S(2)}) collective-permute-start(bf16[64,2176]{1,0:T(8,128)(2,1)S(1)} %get-tuple-element.24.g), channel_id=1, source_target_pairs={{31,0},{0,1},{1,2},{2,3},{3,4},{4,5},{5,6},{6,7},{7,8},{8,9},{9,10... | collective-permute-start | bytes 835592 | tf_op jit(solution)/shard_map/ppermute | solution.py:346
  8.8 9.3 %collective-permute-start.2 = (bf16[64,2176]{1,0:T(8,128)(2,1)S(1)}, bf16[64,2176]{1,0:T(8,128)(2,1)S(1)}, u32[]{:S(2)}, u32[]{:S(2)}) collective-permute-start(bf16[64,2176]{1,0:T(8,128)(2,1)S(1)} %get-tuple-element.31.message), channel_id=1, source_target_pairs={{1,0},{2,1},{3,2},{4,3},{5,4},{6,5},{7,6},{8,7},{9,8},{10,9},{11,1... | collective-permute-start | bytes 835592 | tf_op jit(solution)/shard_map/ppermute | solution.py:346
  15.7 5.9 %collective-permute-start.3 = (bf16[64,2048]{1,0:T(8,128)(2,1)S(1)}, bf16[64,2048]{1,0:T(8,128)(2,1)S(1)}, u32[]{:S(2)}, u32[]{:S(2)}) collective-permute-start(bf16[64,2048]{1,0:T(8,128)(2,1)S(1)} %get-tuple-element.39), channel_id=1, source_target_pairs={{1,0},{2,1},{3,2},{4,3},{5,4},{6,5},{7,6},{8,7},{9,8},{10,9},{11,1... | collective-permute-start | bytes 786440 | tf_op jit(solution)/shard_map/ppermute | solution.py:346
